TPU v7x, 32 devices: a whole 2x2x4 slice. The times are simulated.
32 devices in a mesh: gx: 2 (over x), gy: 4 (over y, core), gz: 4 (over z).
Axes of the slice: x: 2, y: 2, z: 4, core: 2. Of those that a mesh axis runs over, the one named last changes fastest.
Arguments:
- rhs: bfloat16 [16, 32768], P(None, ('gx', 'gy', 'gz')), may hold values from -6 to 6
- leaf_basis: bfloat16 [128, 64, 256], P(('gx', 'gy', 'gz')), may hold values from -0.375 to 0.375
- leaf_transfer: bfloat16 [128, 64, 64], P(('gx', 'gy', 'gz')), may hold values from -0.375 to 0.375
- leaf_coupling: bfloat16 [128, 6, 64, 64], P(('gx', 'gy', 'gz')), may hold values from -0.3125 to 0.3125
- coupling_sources: int32 [128, 6], P(('gx', 'gy', 'gz')), may hold values from -1 to 127, as said below
- near_tiles: bfloat16 [128, 3, 256, 256], P(('gx', 'gy', 'gz')), may hold values from -0.21875 to 0.21875
- near_sources: int32 [128, 3], P(('gx', 'gy', 'gz')), may hold values from -1 to 127, as said below
- top_transfer: bfloat16 [4, 2, 64, 64], replicated, may hold values from -0.625 to 0.625
- cluster_coupling: bfloat16 [5, 2, 64, 64], replicated, may hold values from -0.5 to 0.5
Outputs:
- product: bfloat16 [16, 32768], P(None, ('gx', 'gy', 'gz'))
Inputs may be any that keep to these rules, and one draw needn't show every extreme that they name: `near_sources`: slot 0 of each leaf is the leaf itself; every other entry is -1 (no block) or a leaf at most 2 places from its target leaf in the global order. `coupling_sources`: each entry is -1 (no block) or a leaf other than the target, at most 2 places from it in the global order.
All inputs are finite; a program needn't handle non-finite values.
Results may differ from a plain program's by a relative error of at most 0.0043.
Values may be sent and summed in bfloat16 or wider, within the bound.
A program may use at most 64 MiB of HBM per device.

v0:
```python
import jax
import jax.numpy as jnp
from jax import lax
from jax.sharding import PartitionSpec as P

LEAF = 256
NRHS = 16
TOPL = 4


def extended(cells, sides, width):
    for axis, dim in sides:
        count = lax.axis_size(axis)
        ends = count - 1
        head = lax.slice_in_dim(cells, 0, width, axis=dim)
        tail = lax.slice_in_dim(cells, cells.shape[dim] - width, cells.shape[dim], axis=dim)
        cells = jnp.concatenate(
            [
                lax.ppermute(tail, axis, [(i, (i + 1) % count) for i in range(ends)]),
                cells,
                lax.ppermute(head, axis, [((i + 1) % count, i) for i in range(ends)]),
            ],
            axis=dim,
        )
    return cells


def swapped(shard, axis, stride):
    return lax.ppermute(shard, axis, [(i, i ^ 1 << stride) for i in range(lax.axis_size(axis))])


def passed_along(block, axis, distance):
    devices = range(lax.axis_size(axis))
    route = [(i - distance, i) for i in devices if i - distance in devices]
    return lax.ppermute(block, axis, route)


def parity_matrix(mats, parity, flipped):
    first = mats[0]
    second = mats[1]
    if flipped:
        return jnp.where(parity == 0, second, first)
    return jnp.where(parity == 0, first, second)


def local(
    rhs,
    leaf_basis,
    leaf_transfer,
    leaf_coupling,
    coupling_sources,
    near_tiles,
    near_sources,
    top_transfer,
    cluster_coupling,
):
    exact = lax.Precision.HIGHEST
    dev_index = lax.axis_index(("gx", "gy", "gz"))
    leaf_count = leaf_basis.shape[0]
    span = leaf_count + 2 * leaf_count
    anchor = dev_index * leaf_count - leaf_count

    def local_pick(wide, sources, axis_at):
        position = jnp.clip(sources - anchor, 0, span - 1)
        return (jnp.take(wide, position, axis=axis_at), sources >= 0)

    wide_rhs = extended(rhs, ((("gx", "gy", "gz"), 1),), leaf_count * LEAF)
    wide_rhs = wide_rhs.reshape(NRHS, span, LEAF)
    blocks = rhs.reshape(NRHS, leaf_count, LEAF)
    coeffs = jnp.einsum(
        "rts,tks->trk", blocks, leaf_basis, preferred_element_type=jnp.float32
    ).astype(jnp.bfloat16)
    coeff_wide = extended(coeffs, ((("gx", "gy", "gz"), 0),), leaf_count)
    picked, usable = local_pick(coeff_wide, coupling_sources, 0)
    picked = jnp.where(usable[:, :, None, None], picked, jnp.zeros((), jnp.bfloat16))
    leaf_field = jnp.einsum(
        "tark,takm->trm", picked, leaf_coupling, preferred_element_type=jnp.float32
    )
    root_coeff = jnp.einsum(
        "trk,tkm->rm", coeffs, leaf_transfer, preferred_element_type=jnp.float32
    )
    up_mats = top_transfer.astype(jnp.float32)
    coupling_mats = cluster_coupling.astype(jnp.float32)
    fields = []
    climbed = [root_coeff]
    for height in range(1, TOPL + 1):
        partner = swapped(climbed[-1], ("gx", "gy", "gz"), height - 1)
        parity = dev_index >> height - 1 & 1
        own_mat = parity_matrix(up_mats[height - 1], parity, False)
        other_mat = parity_matrix(up_mats[height - 1], parity, True)
        climbed.append(
            jnp.dot(climbed[-1], own_mat, precision=exact)
            + jnp.dot(partner, other_mat, precision=exact)
        )
    for height in range(TOPL + 1):
        stride = 2**height
        lower_side = passed_along(climbed[height], ("gx", "gy", "gz"), stride)
        upper_side = passed_along(climbed[height], ("gx", "gy", "gz"), -stride)
        fields.append(
            jnp.dot(lower_side, coupling_mats[height, 0], precision=exact)
            + jnp.dot(upper_side, coupling_mats[height, 1], precision=exact)
        )
    incoming = fields[TOPL]
    for height in range(TOPL, 0, -1):
        parity = dev_index >> height - 1 & 1
        own_mat = parity_matrix(up_mats[height - 1], parity, False)
        incoming = fields[height - 1] + jnp.dot(incoming, own_mat.T, precision=exact)
    spread = jnp.einsum("rm,tkm->trk", incoming, leaf_transfer.astype(jnp.float32), precision=exact)
    potential = (leaf_field + spread).astype(jnp.bfloat16)
    far_part = jnp.einsum("trk,tks->rts", potential, leaf_basis, preferred_element_type=jnp.float32)
    near_in, near_ok = local_pick(wide_rhs, near_sources, 1)
    near_in = jnp.where(near_ok[None, :, :, None], near_in, jnp.zeros((), jnp.bfloat16))
    near_part = jnp.einsum(
        "rtns,tnsu->rtu", near_in, near_tiles, preferred_element_type=jnp.float32
    )
    return (far_part + near_part).reshape(NRHS, leaf_count * LEAF).astype(jnp.bfloat16)


def solution(mesh):
    placed = (
        P(None, ("gx", "gy", "gz")),
        P(("gx", "gy", "gz"), None, None),
        P(("gx", "gy", "gz"), None, None),
        P(("gx", "gy", "gz"), None, None, None),
        P(("gx", "gy", "gz"), None),
        P(("gx", "gy", "gz"), None, None, None),
        P(("gx", "gy", "gz"), None),
        P(),
        P(),
    )
    return jax.shard_map(
        local, mesh=mesh, in_specs=placed, out_specs=P(None, ("gx", "gy", "gz")), check_vma=False
    )
```

profile of v0, /device:TPU:2, one launch (start us, length us, event | category | flops | bytes accessed | tf_op | source)
XLA Modules:
  0.0 80.9 jit_solution(12570634141678094888)
XLA Ops:
  0.0 1.2 %convolution_convert_fusion = bf16[4,16,64]{2,1,0:T(8,128)(2,1)S(1)} fusion(bf16[4,64,256]{2,1,0:T(8,128)(2,1)} %param.10, bf16[2,4,8,256]{3,2,1,0:T(8,128)(2,1)} %bitcast.135), kind=kOutput, calls=%fused_computation.10 | convolution fusion | flops 2101248 | bytes 172032 | tf_op jit(solution)/shard_map/rts,tks->trk/dot_general | solution.py:70
  1.2 1.0 %convolution_bitcast_fusion.3 = f32[16,64]{1,0:T(8,128)S(1)} fusion(bf16[4,16,64]{2,1,0:T(8,128)(2,1)S(1)} %convolution_convert_fusion, bf16[4,64,64]{2,1,0:T(8,128)(2,1)} %param.11), kind=kOutput, calls=%fused_computation.25 | convolution fusion | flops 524288 | bytes 45056 | tf_op jit(solution)/shard_map/trk,tkm->rm/dot_general | solution.py:79
  2.3 1.6 %collective-permute-start.4 = (f32[16,64]{1,0:T(8,128)S(1)}, f32[16,64]{1,0:T(8,128)S(1)}, u32[]{:S(2)}, u32[]{:S(2)}) collective-permute-start(f32[16,64]{1,0:T(8,128)S(1)} %convolution_bitcast_fusion.3), channel_id=1, source_target_pairs={{0,1},{1,0},{2,3},{3,2},{4,5},{5,4},{6,7},{7,6},{8,9},{9,8},{10,11... | collective-permute-start | bytes 12296 | tf_op jit(solution)/shard_map/ppermute | solution.py:29
  3.8 4.5 %collective-permute-start.3 = (f32[16,64]{1,0:T(8,128)S(1)}, f32[16,64]{1,0:T(8,128)S(1)}, u32[]{:S(2)}, u32[]{:S(2)}) collective-permute-start(f32[16,64]{1,0:T(8,128)S(1)} %convolution_bitcast_fusion.3), channel_id=1, source_target_pairs={{1,0},{2,1},{3,2},{4,3},{5,4},{6,5},{7,6},{8,7},{9,8},{10,9},{11,1... | collective-permute-start | bytes 12296 | tf_op jit(solution)/shard_map/ppermute | solution.py:35
  8.3 1.9 %collective-permute-start.2 = (f32[16,64]{1,0:T(8,128)S(1)}, f32[16,64]{1,0:T(8,128)S(1)}, u32[]{:S(2)}, u32[]{:S(2)}) collective-permute-start(f32[16,64]{1,0:T(8,128)S(1)} %convolution_bitcast_fusion.3), channel_id=1, source_target_pairs={{0,1},{1,2},{2,3},{3,4},{4,5},{5,6},{6,7},{7,8},{8,9},{9,10},{10,1... | collective-permute-start | bytes 12296 | tf_op jit(solution)/shard_map/ppermute | solution.py:35
  10.2 2.5 %collective-permute-start = (bf16[4,16,64]{2,1,0:T(8,128)(2,1)S(1)}, bf16[4,16,64]{2,1,0:T(8,128)(2,1)S(1)}, u32[]{:S(2)}, u32[]{:S(2)}) collective-permute-start(bf16[4,16,64]{2,1,0:T(8,128)(2,1)S(1)} %convolution_convert_fusion), channel_id=1, source_target_pairs={{0,1},{1,2},{2,3},{3,4},{4,5},{5,6},{6,7},{7,8},{8,9},{9,10},{10,1... | collective-permute-start | bytes 24584 | tf_op jit(solution)/shard_map/ppermute | solution.py:19
  12.7 6.7 %collective-permute-start.1 = (bf16[4,16,64]{2,1,0:T(8,128)(2,1)S(1)}, bf16[4,16,64]{2,1,0:T(8,128)(2,1)S(1)}, u32[]{:S(2)}, u32[]{:S(2)}) collective-permute-start(bf16[4,16,64]{2,1,0:T(8,128)(2,1)S(1)} %convolution_convert_fusion), channel_id=1, source_target_pairs={{1,0},{2,1},{3,2},{4,3},{5,4},{6,5},{7,6},{8,7},{9,8},{10,9},{11,1... | collective-permute-start | bytes 24584 | tf_op jit(solution)/shard_map/ppermute | solution.py:21
  19.4 0.9 %convert_element_type.21 = f32[4,2,64,64]{3,2,1,0:T(8,128)S(1)} convert(bf16[4,2,64,64]{3,2,1,0:T(8,128)(2,1)} %param.16) | non-fusion elementwise | flops 32768 | bytes 196608 | tf_op jit(solution)/shard_map/convert_element_type | solution.py:82
  20.4 0.7 compare_and_fusion.1
  21.1 0.1 reshape.56
  21.1 0.7 compare_and_fusion
  21.8 0.1 reshape.64
  21.9 0.1 fusion.43
  22.1 1.9 %collective-permute-start.16 = (bf16[16,1024]{1,0:T(8,128)(2,1)}, bf16[16,1024]{1,0:T(8,128)(2,1)S(1)}, u32[]{:S(2)}, u32[]{:S(2)}) collective-permute-start(bf16[16,1024]{1,0:T(8,128)(2,1)} %param.9), channel_id=1, source_target_pairs={{0,1},{1,2},{2,3},{3,4},{4,5},{5,6},{6,7},{7,8},{8,9},{9,10},{10,1... | collective-permute-start | bytes 98312 | tf_op jit(solution)/shard_map/ppermute | solution.py:19
  24.0 0.1 convolution_add_fusion.7
  24.2 0.1 fusion.38
  24.3 0.7 collective-permute-start.7
  25.1 0.8 %fusion.69 = f32[16,64]{1,0:T(8,128)S(1)} fusion(f32[16,64]{1,0:T(8,128)S(1)} %collective-permute-done.3, bf16[5,2,64,64]{3,2,1,0:T(8,128)(2,1)} %param.17), kind=kOutput, calls=%fused_computation.92 | convolution fusion | flops 786432 | bytes 24576 | tf_op jit(solution)/shard_map/dot_general | solution.py:101
  25.9 3.1 %collective-permute-done.7 = f32[16,64]{1,0:T(8,128)S(1)} collective-permute-done((f32[16,64]{1,0:T(8,128)S(1)}, f32[16,64]{1,0:T(8,128)S(1)}, u32[]{:S(2)}, u32[]{:S(2)}) %collective-permute-start.7) | collective-permute-done | bytes 4128 | tf_op jit(solution)/shard_map/ppermute | solution.py:29
  29.0 6.0 %collective-permute-start.17 = (bf16[16,1024]{1,0:T(8,128)(2,1)}, bf16[16,1024]{1,0:T(8,128)(2,1)S(1)}, u32[]{:S(2)}, u32[]{:S(2)}) collective-permute-start(bf16[16,1024]{1,0:T(8,128)(2,1)} %param.9), channel_id=1, source_target_pairs={{1,0},{2,1},{3,2},{4,3},{5,4},{6,5},{7,6},{8,7},{9,8},{10,9},{11,1... | collective-permute-start | bytes 98312 | tf_op jit(solution)/shard_map/ppermute | solution.py:21
  35.0 0.1 convolution_add_fusion.5
  35.2 0.1 fusion.33
  35.3 1.9 %collective-permute-start.6 = (f32[16,64]{1,0:T(8,128)S(1)}, f32[16,64]{1,0:T(8,128)S(1)}, u32[]{:S(2)}, u32[]{:S(2)}) collective-permute-start(f32[16,64]{1,0:T(8,128)S(1)} %convolution_add_fusion.7), channel_id=1, source_target_pairs={{2,0},{3,1},{4,2},{5,3},{6,4},{7,5},{8,6},{9,7},{10,8},{11,9},{12,... | collective-permute-start | bytes 12296 | tf_op jit(solution)/shard_map/ppermute | solution.py:35
  37.3 4.8 %collective-permute-start.5 = (f32[16,64]{1,0:T(8,128)S(1)}, f32[16,64]{1,0:T(8,128)S(1)}, u32[]{:S(2)}, u32[]{:S(2)}) collective-permute-start(f32[16,64]{1,0:T(8,128)S(1)} %convolution_add_fusion.7), channel_id=1, source_target_pairs={{0,2},{1,3},{2,4},{3,5},{4,6},{5,7},{6,8},{7,9},{8,10},{9,11},{10,... | collective-permute-start | bytes 12296 | tf_op jit(solution)/shard_map/ppermute | solution.py:35
  42.1 0.6 gather_fusion
  42.7 0.1 collective-permute-start.10
  42.8 0.8 %fusion.66 = f32[16,64]{1,0:T(8,128)S(1)} fusion(f32[16,64]{1,0:T(8,128)S(1)} %collective-permute-done.6, bf16[5,2,64,64]{3,2,1,0:T(8,128)(2,1)} %param.17), kind=kOutput, calls=%fused_computation.89 | convolution fusion | flops 786432 | bytes 24576 | tf_op jit(solution)/shard_map/dot_general | solution.py:101
  43.6 1.3 %convolution_bitcast_fusion.2 = f32[4,16,64]{2,1,0:T(8,128)S(1)} fusion(bf16[4,6,64,64]{3,2,1,0:T(8,128)(2,1)} %param.12, bf16[4,6,16,64]{3,2,1,0:T(8,128)(2,1)S(1)} %bitcast.136, pred[4,6]{1,0:T(4,128)(4,1)S(1)} %get-tuple-element.7, pred[4,6]{1,0:T(4,128)(4,1)S(1)} %get-tuple-element.10), kind=kOutput, calls=%fused_computation.8 | convolution fusion | flops 3194880 | bytes 262192 | tf_op jit(solution)/shard_map/tark,takm->trm/dot_general | solution.py:76
  45.0 1.9 %collective-permute-start.9 = (f32[16,64]{1,0:T(8,128)S(1)}, f32[16,64]{1,0:T(8,128)S(1)}, u32[]{:S(2)}, u32[]{:S(2)}) collective-permute-start(f32[16,64]{1,0:T(8,128)S(1)} %convolution_add_fusion.5), channel_id=1, source_target_pairs={{4,0},{5,1},{6,2},{7,3},{8,4},{9,5},{10,6},{11,7},{12,8},{13,9},{1... | collective-permute-start | bytes 12296 | tf_op jit(solution)/shard_map/ppermute | solution.py:35
  46.9 0.1 convolution_add_fusion.3
  47.1 0.1 fusion.28
  47.2 1.1 %collective-permute-done.9 = f32[16,64]{1,0:T(8,128)S(1)} collective-permute-done((f32[16,64]{1,0:T(8,128)S(1)}, f32[16,64]{1,0:T(8,128)S(1)}, u32[]{:S(2)}, u32[]{:S(2)}) %collective-permute-start.9) | collective-permute-done | bytes 4128 | tf_op jit(solution)/shard_map/ppermute | solution.py:35
  48.3 2.1 %collective-permute-start.13 = (f32[16,64]{1,0:T(8,128)S(1)}, f32[16,64]{1,0:T(8,128)S(1)}, u32[]{:S(2)}, u32[]{:S(2)}) collective-permute-start(f32[16,64]{1,0:T(8,128)S(1)} %convolution_add_fusion.3), channel_id=1, source_target_pairs={{0,8},{1,9},{2,10},{3,11},{4,12},{5,13},{6,14},{7,15},{8,0},{9,1},... | collective-permute-start | bytes 12296 | tf_op jit(solution)/shard_map/ppermute | solution.py:29
  50.4 0.1 fusion.63
  50.5 1.5 %collective-permute-done.13 = f32[16,64]{1,0:T(8,128)S(1)} collective-permute-done((f32[16,64]{1,0:T(8,128)S(1)}, f32[16,64]{1,0:T(8,128)S(1)}, u32[]{:S(2)}, u32[]{:S(2)}) %collective-permute-start.13) | collective-permute-done | bytes 4128 | tf_op jit(solution)/shard_map/ppermute | solution.py:29
  52.0 1.9 %collective-permute-start.12 = (f32[16,64]{1,0:T(8,128)S(1)}, f32[16,64]{1,0:T(8,128)S(1)}, u32[]{:S(2)}, u32[]{:S(2)}) collective-permute-start(f32[16,64]{1,0:T(8,128)S(1)} %convolution_add_fusion.3), channel_id=1, source_target_pairs={{8,0},{9,1},{10,2},{11,3},{12,4},{13,5},{14,6},{15,7},{16,8},{17,9... | collective-permute-start | bytes 12296 | tf_op jit(solution)/shard_map/ppermute | solution.py:35
  53.9 0.1 convolution_add_fusion.1
  54.1 3.5 %collective-permute-done.12 = f32[16,64]{1,0:T(8,128)S(1)} collective-permute-done((f32[16,64]{1,0:T(8,128)S(1)}, f32[16,64]{1,0:T(8,128)S(1)}, u32[]{:S(2)}, u32[]{:S(2)}) %collective-permute-start.12) | collective-permute-done | bytes 4128 | tf_op jit(solution)/shard_map/ppermute | solution.py:35
  57.6 1.3 %collective-permute-start.15 = (f32[16,64]{1,0:T(8,128)S(1)}, f32[16,64]{1,0:T(8,128)S(1)}, u32[]{:S(2)}, u32[]{:S(2)}) collective-permute-start(f32[16,64]{1,0:T(8,128)S(1)} %convolution_add_fusion.1), channel_id=1, source_target_pairs={{16,0},{17,1},{18,2},{19,3},{20,4},{21,5},{22,6},{23,7},{24,8},{25... | collective-permute-start | bytes 12296 | tf_op jit(solution)/shard_map/ppermute | solution.py:35
  58.9 0.1 fusion.60
  59.0 1.2 %collective-permute-done.15 = f32[16,64]{1,0:T(8,128)S(1)} collective-permute-done((f32[16,64]{1,0:T(8,128)S(1)}, f32[16,64]{1,0:T(8,128)S(1)}, u32[]{:S(2)}, u32[]{:S(2)}) %collective-permute-start.15) | collective-permute-done | bytes 4128 | tf_op jit(solution)/shard_map/ppermute | solution.py:35
  60.2 1.3 %collective-permute-start.14 = (f32[16,64]{1,0:T(8,128)S(1)}, f32[16,64]{1,0:T(8,128)S(1)}, u32[]{:S(2)}, u32[]{:S(2)}) collective-permute-start(f32[16,64]{1,0:T(8,128)S(1)} %convolution_add_fusion.1), channel_id=1, source_target_pairs={{0,16},{1,17},{2,18},{3,19},{4,20},{5,21},{6,22},{7,23},{8,24},{9,... | collective-permute-start | bytes 12296 | tf_op jit(solution)/shard_map/ppermute | solution.py:35
  61.5 0.1 fusion.57
  61.7 4.1 %collective-permute-done.14 = f32[16,64]{1,0:T(8,128)S(1)} collective-permute-done((f32[16,64]{1,0:T(8,128)S(1)}, f32[16,64]{1,0:T(8,128)S(1)}, u32[]{:S(2)}, u32[]{:S(2)}) %collective-permute-start.14) | collective-permute-done | bytes 4128 | tf_op jit(solution)/shard_map/ppermute | solution.py:35
  65.8 3.9 %collective-permute-start.11 = (f32[16,64]{1,0:T(8,128)S(1)}, f32[16,64]{1,0:T(8,128)S(1)}, u32[]{:S(2)}, u32[]{:S(2)}) collective-permute-start(f32[16,64]{1,0:T(8,128)S(1)} %convolution_add_fusion.3), channel_id=1, source_target_pairs={{0,8},{1,9},{2,10},{3,11},{4,12},{5,13},{6,14},{7,15},{8,16},{9,17... | collective-permute-start | bytes 12296 | tf_op jit(solution)/shard_map/ppermute | solution.py:35
  69.7 0.1 convolution_add_fusion
  69.8 0.2 fusion.26
  70.0 2.2 %collective-permute-done.11 = f32[16,64]{1,0:T(8,128)S(1)} collective-permute-done((f32[16,64]{1,0:T(8,128)S(1)}, f32[16,64]{1,0:T(8,128)S(1)}, u32[]{:S(2)}, u32[]{:S(2)}) %collective-permute-start.11) | collective-permute-done | bytes 4128 | tf_op jit(solution)/shard_map/ppermute | solution.py:35
  72.2 1.9 %collective-permute-start.8 = (f32[16,64]{1,0:T(8,128)S(1)}, f32[16,64]{1,0:T(8,128)S(1)}, u32[]{:S(2)}, u32[]{:S(2)}) collective-permute-start(f32[16,64]{1,0:T(8,128)S(1)} %convolution_add_fusion.5), channel_id=1, source_target_pairs={{0,4},{1,5},{2,6},{3,7},{4,8},{5,9},{6,10},{7,11},{8,12},{9,13},{1... | collective-permute-start | bytes 12296 | tf_op jit(solution)/shard_map/ppermute | solution.py:35
  74.1 0.1 fusion.5
  74.3 0.2 fusion.31
  74.4 3.7 %collective-permute-done.8 = f32[16,64]{1,0:T(8,128)S(1)} collective-permute-done((f32[16,64]{1,0:T(8,128)S(1)}, f32[16,64]{1,0:T(8,128)S(1)}, u32[]{:S(2)}, u32[]{:S(2)}) %collective-permute-start.8) | collective-permute-done | bytes 4128 | tf_op jit(solution)/shard_map/ppermute | solution.py:35
  78.1 0.1 fusion.6
  78.2 0.2 fusion.36
  78.3 0.0 collective-permute-done.5
  78.4 0.1 fusion.7
  78.5 0.2 fusion.41
  78.7 0.0 collective-permute-done.2
  78.7 0.1 fusion.9
  78.8 0.3 fusion.4
  79.1 0.1 fusion.90
  79.3 0.6 gather_fusion.1
  79.9 0.4 fusion.2
  80.2 0.6 copy.19
  (23 shorter events, 0.1 us)
Async XLA Ops:
  0.0 79.9 %copy-start = (bf16[4,3,256,256]{3,2,1,0:T(8,128)(2,1)S(1)}, bf16[4,3,256,256]{3,2,1,0:T(8,128)(2,1)}, u32[]{:S(2)}) copy-start(bf16[4,3,256,256]{3,2,1,0:T(8,128)(2,1)} %param.14) | copy-start | bytes 4718596
  0.0 79.3 %copy-start.4 = (bf16[16,1024]{1,0:T(8,128)(2,1)S(1)}, bf16[16,1024]{1,0:T(8,128)(2,1)}, u32[]{:S(2)}) copy-start(bf16[16,1024]{1,0:T(8,128)(2,1)} %param.9) | copy-start | bytes 98308
  0.0 79.1 %copy-start.1 = (bf16[4,64,256]{2,1,0:T(8,128)(2,1)S(1)}, bf16[4,64,256]{2,1,0:T(8,128)(2,1)}, u32[]{:S(2)}) copy-start(bf16[4,64,256]{2,1,0:T(8,128)(2,1)} %param.10) | copy-start | bytes 393220
  0.0 78.8 %copy-start.2 = (bf16[4,64,64]{2,1,0:T(8,128)(2,1)S(1)}, bf16[4,64,64]{2,1,0:T(8,128)(2,1)}, u32[]{:S(2)}) copy-start(bf16[4,64,64]{2,1,0:T(8,128)(2,1)} %param.11) | copy-start | bytes 98308
  0.0 50.4 %copy-start.3 = (bf16[5,2,64,64]{3,2,1,0:T(8,128)(2,1)S(1)}, bf16[5,2,64,64]{3,2,1,0:T(8,128)(2,1)}, u32[]{:S(2)}) copy-start(bf16[5,2,64,64]{3,2,1,0:T(8,128)(2,1)} %param.17) | copy-start | bytes 245764
  2.3 19.8 %collective-permute-start.4 = (f32[16,64]{1,0:T(8,128)S(1)}, f32[16,64]{1,0:T(8,128)S(1)}, u32[]{:S(2)}, u32[]{:S(2)}) collective-permute-start(f32[16,64]{1,0:T(8,128)S(1)} %convolution_bitcast_fusion.3), channel_id=1, source_target_pairs={{0,1},{1,0},{2,3},{3,2},{4,5},{5,4},{6,7},{7,6},{8,9},{9,8},{10,11... | collective-permute-start | bytes 12296 | tf_op jit(solution)/shard_map/ppermute | solution.py:29
  3.8 20.5 %collective-permute-start.3 = (f32[16,64]{1,0:T(8,128)S(1)}, f32[16,64]{1,0:T(8,128)S(1)}, u32[]{:S(2)}, u32[]{:S(2)}) collective-permute-start(f32[16,64]{1,0:T(8,128)S(1)} %convolution_bitcast_fusion.3), channel_id=1, source_target_pairs={{1,0},{2,1},{3,2},{4,3},{5,4},{6,5},{7,6},{8,7},{9,8},{10,9},{11,1... | collective-permute-start | bytes 12296 | tf_op jit(solution)/shard_map/ppermute | solution.py:35
  8.3 70.4 %collective-permute-start.2 = (f32[16,64]{1,0:T(8,128)S(1)}, f32[16,64]{1,0:T(8,128)S(1)}, u32[]{:S(2)}, u32[]{:S(2)}) collective-permute-start(f32[16,64]{1,0:T(8,128)S(1)} %convolution_bitcast_fusion.3), channel_id=1, source_target_pairs={{0,1},{1,2},{2,3},{3,4},{4,5},{5,6},{6,7},{7,8},{8,9},{9,10},{10,1... | collective-permute-start | bytes 12296 | tf_op jit(solution)/shard_map/ppermute | solution.py:35
  10.2 25.1 %collective-permute-start = (bf16[4,16,64]{2,1,0:T(8,128)(2,1)S(1)}, bf16[4,16,64]{2,1,0:T(8,128)(2,1)S(1)}, u32[]{:S(2)}, u32[]{:S(2)}) collective-permute-start(bf16[4,16,64]{2,1,0:T(8,128)(2,1)S(1)} %convolution_convert_fusion), channel_id=1, source_target_pairs={{0,1},{1,2},{2,3},{3,4},{4,5},{5,6},{6,7},{7,8},{8,9},{9,10},{10,1... | collective-permute-start | bytes 24584 | tf_op jit(solution)/shard_map/ppermute | solution.py:19
  12.7 24.5 %collective-permute-start.1 = (bf16[4,16,64]{2,1,0:T(8,128)(2,1)S(1)}, bf16[4,16,64]{2,1,0:T(8,128)(2,1)S(1)}, u32[]{:S(2)}, u32[]{:S(2)}) collective-permute-start(bf16[4,16,64]{2,1,0:T(8,128)(2,1)S(1)} %convolution_convert_fusion), channel_id=1, source_target_pairs={{1,0},{2,1},{3,2},{4,3},{5,4},{6,5},{7,6},{8,7},{9,8},{10,9},{11,1... | collective-permute-start | bytes 24584 | tf_op jit(solution)/shard_map/ppermute | solution.py:21
  22.1 57.1 %collective-permute-start.16 = (bf16[16,1024]{1,0:T(8,128)(2,1)}, bf16[16,1024]{1,0:T(8,128)(2,1)S(1)}, u32[]{:S(2)}, u32[]{:S(2)}) collective-permute-start(bf16[16,1024]{1,0:T(8,128)(2,1)} %param.9), channel_id=1, source_target_pairs={{0,1},{1,2},{2,3},{3,4},{4,5},{5,6},{6,7},{7,8},{8,9},{9,10},{10,1... | collective-permute-start | bytes 98312 | tf_op jit(solution)/shard_map/ppermute | solution.py:19
  24.3 4.7 %collective-permute-start.7 = (f32[16,64]{1,0:T(8,128)S(1)}, f32[16,64]{1,0:T(8,128)S(1)}, u32[]{:S(2)}, u32[]{:S(2)}) collective-permute-start(f32[16,64]{1,0:T(8,128)S(1)} %convolution_add_fusion.7), channel_id=1, source_target_pairs={{0,2},{1,3},{2,0},{3,1},{4,6},{5,7},{6,4},{7,5},{8,10},{9,11},{10,... | collective-permute-start | bytes 12296 | tf_op jit(solution)/shard_map/ppermute | solution.py:29
  29.0 50.2 %collective-permute-start.17 = (bf16[16,1024]{1,0:T(8,128)(2,1)}, bf16[16,1024]{1,0:T(8,128)(2,1)S(1)}, u32[]{:S(2)}, u32[]{:S(2)}) collective-permute-start(bf16[16,1024]{1,0:T(8,128)(2,1)} %param.9), channel_id=1, source_target_pairs={{1,0},{2,1},{3,2},{4,3},{5,4},{6,5},{7,6},{8,7},{9,8},{10,9},{11,1... | collective-permute-start | bytes 98312 | tf_op jit(solution)/shard_map/ppermute | solution.py:21
  35.3 7.4 %collective-permute-start.6 = (f32[16,64]{1,0:T(8,128)S(1)}, f32[16,64]{1,0:T(8,128)S(1)}, u32[]{:S(2)}, u32[]{:S(2)}) collective-permute-start(f32[16,64]{1,0:T(8,128)S(1)} %convolution_add_fusion.7), channel_id=1, source_target_pairs={{2,0},{3,1},{4,2},{5,3},{6,4},{7,5},{8,6},{9,7},{10,8},{11,9},{12,... | collective-permute-start | bytes 12296 | tf_op jit(solution)/shard_map/ppermute | solution.py:35
  37.3 41.1 %collective-permute-start.5 = (f32[16,64]{1,0:T(8,128)S(1)}, f32[16,64]{1,0:T(8,128)S(1)}, u32[]{:S(2)}, u32[]{:S(2)}) collective-permute-start(f32[16,64]{1,0:T(8,128)S(1)} %convolution_add_fusion.7), channel_id=1, source_target_pairs={{0,2},{1,3},{2,4},{3,5},{4,6},{5,7},{6,8},{7,9},{8,10},{9,11},{10,... | collective-permute-start | bytes 12296 | tf_op jit(solution)/shard_map/ppermute | solution.py:35
  42.7 2.3 %collective-permute-start.10 = (f32[16,64]{1,0:T(8,128)S(1)}, f32[16,64]{1,0:T(8,128)S(1)}, u32[]{:S(2)}, u32[]{:S(2)}) collective-permute-start(f32[16,64]{1,0:T(8,128)S(1)} %convolution_add_fusion.5), channel_id=1, source_target_pairs={{0,4},{1,5},{2,6},{3,7},{4,0},{5,1},{6,2},{7,3},{8,12},{9,13},{10,... | collective-permute-start | bytes 12296 | tf_op jit(solution)/shard_map/ppermute | solution.py:29
  45.0 3.3 %collective-permute-start.9 = (f32[16,64]{1,0:T(8,128)S(1)}, f32[16,64]{1,0:T(8,128)S(1)}, u32[]{:S(2)}, u32[]{:S(2)}) collective-permute-start(f32[16,64]{1,0:T(8,128)S(1)} %convolution_add_fusion.5), channel_id=1, source_target_pairs={{4,0},{5,1},{6,2},{7,3},{8,4},{9,5},{10,6},{11,7},{12,8},{13,9},{1... | collective-permute-start | bytes 12296 | tf_op jit(solution)/shard_map/ppermute | solution.py:35
  48.3 3.7 %collective-permute-start.13 = (f32[16,64]{1,0:T(8,128)S(1)}, f32[16,64]{1,0:T(8,128)S(1)}, u32[]{:S(2)}, u32[]{:S(2)}) collective-permute-start(f32[16,64]{1,0:T(8,128)S(1)} %convolution_add_fusion.3), channel_id=1, source_target_pairs={{0,8},{1,9},{2,10},{3,11},{4,12},{5,13},{6,14},{7,15},{8,0},{9,1},... | collective-permute-start | bytes 12296 | tf_op jit(solution)/shard_map/ppermute | solution.py:29
  52.0 5.6 %collective-permute-start.12 = (f32[16,64]{1,0:T(8,128)S(1)}, f32[16,64]{1,0:T(8,128)S(1)}, u32[]{:S(2)}, u32[]{:S(2)}) collective-permute-start(f32[16,64]{1,0:T(8,128)S(1)} %convolution_add_fusion.3), channel_id=1, source_target_pairs={{8,0},{9,1},{10,2},{11,3},{12,4},{13,5},{14,6},{15,7},{16,8},{17,9... | collective-permute-start | bytes 12296 | tf_op jit(solution)/shard_map/ppermute | solution.py:35
  57.6 2.6 %collective-permute-start.15 = (f32[16,64]{1,0:T(8,128)S(1)}, f32[16,64]{1,0:T(8,128)S(1)}, u32[]{:S(2)}, u32[]{:S(2)}) collective-permute-start(f32[16,64]{1,0:T(8,128)S(1)} %convolution_add_fusion.1), channel_id=1, source_target_pairs={{16,0},{17,1},{18,2},{19,3},{20,4},{21,5},{22,6},{23,7},{24,8},{25... | collective-permute-start | bytes 12296 | tf_op jit(solution)/shard_map/ppermute | solution.py:35
  60.2 5.5 %collective-permute-start.14 = (f32[16,64]{1,0:T(8,128)S(1)}, f32[16,64]{1,0:T(8,128)S(1)}, u32[]{:S(2)}, u32[]{:S(2)}) collective-permute-start(f32[16,64]{1,0:T(8,128)S(1)} %convolution_add_fusion.1), channel_id=1, source_target_pairs={{0,16},{1,17},{2,18},{3,19},{4,20},{5,21},{6,22},{7,23},{8,24},{9,... | collective-permute-start | bytes 12296 | tf_op jit(solution)/shard_map/ppermute | solution.py:35
  65.8 6.4 %collective-permute-start.11 = (f32[16,64]{1,0:T(8,128)S(1)}, f32[16,64]{1,0:T(8,128)S(1)}, u32[]{:S(2)}, u32[]{:S(2)}) collective-permute-start(f32[16,64]{1,0:T(8,128)S(1)} %convolution_add_fusion.3), channel_id=1, source_target_pairs={{0,8},{1,9},{2,10},{3,11},{4,12},{5,13},{6,14},{7,15},{8,16},{9,17... | collective-permute-start | bytes 12296 | tf_op jit(solution)/shard_map/ppermute | solution.py:35
  72.2 5.9 %collective-permute-start.8 = (f32[16,64]{1,0:T(8,128)S(1)}, f32[16,64]{1,0:T(8,128)S(1)}, u32[]{:S(2)}, u32[]{:S(2)}) collective-permute-start(f32[16,64]{1,0:T(8,128)S(1)} %convolution_add_fusion.5), channel_id=1, source_target_pairs={{0,4},{1,5},{2,6},{3,7},{4,8},{5,9},{6,10},{7,11},{8,12},{9,13},{1... | collective-permute-start | bytes 12296 | tf_op jit(solution)/shard_map/ppermute | solution.py:35
where the time goes:
time: 81.6 us; the launch traced here: 80.9 us
  starting transfers between devices  46.9 us (57%)
  waiting for transfers between devices  20.5 us (25%)
  matrix products  8.73 us (11%)
  other arithmetic  2.36 us (3%)
  local copies, waits for them, and re-layouts  1.96 us (2%)
    ppermute x10, starting transfers between devices, passed_along(): return lax.ppermute(block, axis, route)  25.3 us
    ppermute x10, waiting for transfers between devices, passed_along(): return lax.ppermute(block, axis, route)  15.9 us
    ppermute x2, starting transfers between devices, extended(): lax.ppermute(head, axis, [((i + 1) % count, i) for i in range(ends)])  12.7 us
    ppermute x4, waiting for transfers between devices, swapped(): lax.ppermute(shard, axis, [(i, i ^ 1 << stride) for i in range(lax.axis_s...  4.62 us
    ppermute x4, starting transfers between devices, swapped(): lax.ppermute(shard, axis, [(i, i ^ 1 << stride) for i in range(lax.axis_s...  4.51 us
    ppermute x2, starting transfers between devices, extended(): lax.ppermute(tail, axis, [(i, (i + 1) % count) for i in range(ends)])  4.42 us
    dot_general x5, matrix products, local(): jnp.dot(upper_side, coupling_mats[height, 1], precision=exact)  2.04 us
  transfers between devices with their start and end apart: 18, of which 8 were waited for; matrix products, arithmetic and copies ran while one was open for 11% of the time, Pallas kernels for 0%

commit v1 on v0

v1 whole, which is shorter than its diff:
```python
import functools

import jax
import jax.numpy as jnp
from jax import lax
from jax.experimental import pallas as pl
from jax.experimental.pallas import tpu as pltpu
from jax.sharding import PartitionSpec as P

AXES = ("gx", "gy", "gz")
REACH = 2
MESH = pl.DeviceIdType.MESH
BF16 = jnp.bfloat16
F32 = jnp.float32


def mm(a, b):
    return jnp.dot(a, b, preferred_element_type=F32)


def mm_nt(a, b):
    return lax.dot_general(a, b, (((1,), (1,)), ((), ())), preferred_element_type=F32)


def mm_tn(a, b):
    return lax.dot_general(a, b, (((0,), (0,)), ((), ())), preferred_element_type=F32)


def kernel(
    shape,
    rhs_h, basis_h, trans_h, coup_h, csrc_h, near_h, nsrc_h, top_h, cc_h,
    out_ref,
    rhs_v, basis_v, trans_v, coup_v, csrc_s, near_v, nsrc_s, top_v, cc_v,
    wide_x, wide_c, slots, part, part_in,
    local_sem, halo_send, halo_recv, p_send, p_recv, r_send, r_recv,
):
    nx, ny, nz = shape
    count = nx * ny * nz
    leaves, rank, leaf = basis_v.shape
    rows = rhs_v.shape[0]
    slots_near = near_v.shape[1]
    slots_adm = coup_v.shape[1]
    topl = top_v.shape[0]
    gsize = 2**topl
    groups = count // gsize
    blocks = part.shape[1] // rank
    width = blocks * rank

    me = (lax.axis_index("gx") * ny + lax.axis_index("gy")) * nz + lax.axis_index("gz")
    group = me // gsize
    rel = me % gsize

    def place(e):
        return (e // (ny * nz), (e // nz) % ny, e % nz)

    loads = []
    for i, (src, dst) in enumerate(
        (
            (rhs_h, rhs_v), (basis_h, basis_v), (trans_h, trans_v), (top_h, top_v),
            (cc_h, cc_v), (csrc_h, csrc_s), (nsrc_h, nsrc_s), (coup_h, coup_v),
            (near_h, near_v),
        )
    ):
        load = pltpu.make_async_copy(src, dst, local_sem.at[i])
        load.start()
        loads.append(load)
    (l_rhs, l_basis, l_trans, l_top, l_cc, l_csrc, l_nsrc, l_coup, l_near) = loads

    if groups == 2:
        across = (((me + gsize) % count, None, 0),)
    else:
        across = ((me - gsize, group > 0, 1), (me + gsize, group < groups - 1, 0))
    has_prev, has_next = me > 0, me < count - 1

    barrier = pltpu.get_barrier_semaphore()

    def greet(e):
        pl.semaphore_signal(barrier, inc=1, device_id=place(e), device_id_type=MESH)

    def when(cond, fn):
        if cond is None:
            fn()
        else:
            pl.when(cond)(fn)

    peers = [group * gsize + (rel + r) % gsize for r in range(1, gsize)]
    for e in peers:
        greet(e)
    expected = jnp.int32(gsize - 1)
    out_prev = has_prev & (rel == 0)
    out_next = has_next & (rel == gsize - 1)
    for e, ok, _ in across:
        when(ok, functools.partial(greet, e))
        expected += 1 if ok is None else ok.astype(jnp.int32)
    for e, ok in ((me - 1, out_prev), (me + 1, out_next)):
        when(ok, functools.partial(greet, e))
        expected += ok.astype(jnp.int32)

    wide_x[leaves + 2 * REACH] = jnp.zeros((rows, leaf), BF16)
    wide_c[leaves + 2 * REACH] = jnp.zeros((rows, 2 * rank), BF16)
    low = lax.broadcasted_iota(jnp.int32, (rows, 2 * rank), 1) < rank

    l_rhs.wait()
    l_basis.wait()
    coeffs = []
    for t in range(leaves):
        block = rhs_v[:, t * leaf:(t + 1) * leaf]
        wide_x[REACH + t] = block
        basis = basis_v[t]
        both = mm_nt(block, jnp.concatenate([basis, basis], 0)).astype(BF16)
        wide_c[REACH + t] = both
        coeffs.append(both)
    pairs = [jnp.where(low, coeffs[t], coeffs[t + 1]) for t in range(0, leaves, 2)]
    l_trans.wait()
    root = mm(jnp.concatenate(pairs, 1), trans_v[...].reshape(leaves * rank, rank)).astype(BF16)
    slots[rel] = jnp.concatenate([root, root], 1)

    pl.semaphore_wait(barrier, expected)

    sends = []
    for e in peers:
        copy = pltpu.make_async_remote_copy(
            src_ref=slots.at[rel], dst_ref=slots.at[rel],
            send_sem=p_send.at[0], recv_sem=p_recv.at[0],
            device_id=place(e), device_id_type=MESH,
        )
        copy.start()

    def halo(buf, i, up):
        first, land = (leaves, 0) if up else (REACH, leaves + REACH)
        return pltpu.make_async_remote_copy(
            src_ref=buf.at[pl.ds(first, REACH)], dst_ref=buf.at[pl.ds(land, REACH)],
            send_sem=halo_send.at[i], recv_sem=halo_recv.at[i],
            device_id=place(me + 1 if up else me - 1), device_id_type=MESH,
        )

    ups = (halo(wide_c, 0, True), halo(wide_x, 1, True))
    downs = (halo(wide_c, 2, False), halo(wide_x, 3, False))

    @pl.when(has_next)
    def _():
        for copy in ups:
            copy.start()

    @pl.when(has_prev)
    def _():
        for copy in downs:
            copy.start()

    l_top.wait()
    l_cc.wait()
    lane_block = lax.broadcasted_iota(jnp.int32, (1, width), 1) // rank
    if groups == 2:
        dest = jnp.where(lane_block == 0, me, (me + gsize) % count)
    else:
        dest = jnp.where(lane_block == 0, me, jnp.where(lane_block == 1, me - gsize, me + gsize))
        dest = jnp.where(lane_block == 3, -8 * gsize, dest)
    row = lax.broadcasted_iota(jnp.int32, (rank, rank), 0)
    col = lax.broadcasted_iota(jnp.int32, (rank, rank), 1)
    down = jnp.where(row == col, 1.0, 0.0).astype(BF16)
    reach_mats = []
    for h in range(topl + 1):
        if h == 1:
            down = top_v[0, rel % 2]
        elif h > 1:
            down = mm(down, top_v[h - 1, (rel // 2 ** (h - 1)) % 2]).astype(BF16)
        reach_mats.append(
            mm_nt(cc_v[h].reshape(2 * rank, rank), jnp.concatenate([down] * blocks, 0))
        )

    def coupled(h, cluster):
        home = dest >> h
        return jnp.where(cluster == home - 1, reach_mats[h][:rank], 0.0) + jnp.where(
            cluster == home + 1, reach_mats[h][rank:], 0.0
        )

    level = [coupled(topl, group)]
    for h in range(topl - 1, -1, -1):
        wide = jnp.concatenate([m.astype(BF16) for m in level], 1)
        grown = mm(top_v[h].reshape(2 * rank, rank), wide)
        first = group * 2 ** (topl - h)
        level = [
            grown[(c % 2) * rank:(c % 2 + 1) * rank, (c // 2) * width:(c // 2 + 1) * width]
            + coupled(h, first + c)
            for c in range(2 ** (topl - h))
        ]
    gather_mat = jnp.concatenate([m.astype(BF16) for m in level], 0)

    spread = [mm_tn(trans_v[t], basis_v[t]).astype(BF16) for t in range(leaves)]
    spread = jnp.concatenate(spread, 1)
    spread = jnp.concatenate([spread] * blocks, 0)

    everyone = pltpu.make_async_copy(
        slots.at[pl.ds(0, gsize - 1)], slots.at[pl.ds(0, gsize - 1)], p_recv.at[0]
    )
    everyone.wait()
    held = [jnp.where(low, slots[c], slots[c + 1]) for c in range(0, gsize, 2)]
    own = mm(jnp.concatenate(held, 1), gather_mat)
    part[...] = own

    def partner(i, e, slot):
        return pltpu.make_async_remote_copy(
            src_ref=part, dst_ref=part_in.at[slot],
            send_sem=r_send.at[i], recv_sem=r_recv.at[slot],
            device_id=place(e), device_id_type=MESH,
        )

    partners = [(partner(i, e, slot), ok) for i, (e, ok, slot) in enumerate(across)]
    for copy, ok in partners:
        when(ok, copy.start)

    l_csrc.wait()
    l_nsrc.wait()
    l_coup.wait()
    l_near.wait()

    @pl.when(has_prev)
    def _():
        for copy in ups:
            copy.wait_recv()

    @pl.when(has_next)
    def _():
        for copy in downs:
            copy.wait_recv()

    anchor = me * leaves - REACH
    last = leaves + 2 * REACH

    def spot(source):
        return jnp.where(source >= 0, jnp.clip(source - anchor, 0, last - 1), last)

    sums = []
    for t in range(leaves):
        picked = [wide_c[spot(csrc_s[t, a])] for a in range(slots_adm)]
        picked = [jnp.where(low, picked[a], picked[a + 1]) for a in range(0, slots_adm, 2)]
        field = mm(
            jnp.concatenate(picked, 1), coup_v[t].reshape(slots_adm * rank, rank)
        ).astype(BF16)
        inputs = [wide_x[REACH + t]]
        inputs += [wide_x[spot(nsrc_s[t, n])] for n in range(1, slots_near)]
        sums.append(
            mm(jnp.concatenate(inputs, 1), near_v[t].reshape(slots_near * leaf, leaf))
            + mm(field, basis_v[t])
        )

    cells = lax.broadcasted_iota(jnp.int32, (rows, width), 1) // rank
    if groups == 2:
        partners[0][0].wait_recv()
        total = jnp.where(cells == 0, own, part_in[0])
    else:
        def arrived(slot, ok):
            pltpu.make_async_copy(part_in.at[slot], part_in.at[slot], r_recv.at[slot]).wait()

        pl.when(group > 0)(functools.partial(arrived, 0, None))
        pl.when(group < groups - 1)(functools.partial(arrived, 1, None))
        total = jnp.where(cells == 0, own, 0.0)
        total = jnp.where((cells == 1) & (group < groups - 1), part_in[1], total)
        total = jnp.where((cells == 2) & (group > 0), part_in[0], total)
    far = mm(total.astype(BF16), spread)
    for t in range(leaves):
        out_ref[:, t * leaf:(t + 1) * leaf] = (
            sums[t] + far[:, t * leaf:(t + 1) * leaf]
        ).astype(BF16)

    pltpu.make_async_copy(
        slots.at[pl.ds(0, gsize - 1)], slots.at[pl.ds(0, gsize - 1)], p_send.at[0]
    ).wait()
    for copy, ok in partners:
        when(ok, copy.wait_send)

    @pl.when(has_next)
    def _():
        for copy in ups:
            copy.wait_send()

    @pl.when(has_prev)
    def _():
        for copy in downs:
            copy.wait_send()


def solution(mesh):
    shape = tuple(mesh.shape[a] for a in AXES)
    count = shape[0] * shape[1] * shape[2]

    def local(rhs, basis, trans, coup, csrc, near, nsrc, top, cc):
        leaves, rank, leaf = basis.shape
        rows = rhs.shape[0]
        gsize = 2 ** top.shape[0]
        blocks = 2 if count == 2 * gsize else 4
        args = (rhs, basis, trans, coup, csrc, near, nsrc, top, cc)

        def room(x):
            kind = pltpu.SMEM if x.dtype == jnp.int32 else pltpu.VMEM
            return kind(x.shape, x.dtype)

        dma = pltpu.SemaphoreType.DMA
        return pl.pallas_call(
            functools.partial(kernel, shape),
            out_shape=jax.ShapeDtypeStruct(rhs.shape, BF16),
            in_specs=[pl.BlockSpec(memory_space=pl.ANY)] * len(args),
            out_specs=pl.BlockSpec(memory_space=pltpu.VMEM),
            scratch_shapes=[room(x) for x in args] + [
                pltpu.VMEM((leaves + 2 * REACH + 1, rows, leaf), BF16),
                pltpu.VMEM((leaves + 2 * REACH + 1, rows, 2 * rank), BF16),
                pltpu.VMEM((gsize, rows, 2 * rank), BF16),
                pltpu.VMEM((rows, blocks * rank), F32),
                pltpu.VMEM((blocks // 2, rows, blocks * rank), F32),
                dma((len(args),)), dma((4,)), dma((4,)), dma((1,)), dma((1,)),
                dma((2,)), dma((2,)),
            ],
            compiler_params=pltpu.CompilerParams(collective_id=0, has_side_effects=True),
        )(*args)

    placed = (
        P(None, AXES),
        P(AXES, None, None),
        P(AXES, None, None),
        P(AXES, None, None, None),
        P(AXES, None),
        P(AXES, None, None, None),
        P(AXES, None),
        P(),
        P(),
    )
    return jax.shard_map(
        local, mesh=mesh, in_specs=placed, out_specs=P(None, AXES), check_vma=False
    )
```

time: 81.6 us -> 15.6 us (0.19)
  the two profiles are of different devices: /device:TPU:2 before, /device:TPU:0 now
where the time goes in v1:
time: 15.6 us; the launch traced here: 15.4 us
  Pallas kernels  14 us (90%)
  local copies, waits for them, and re-layouts  1.38 us (9%)
    pallas_call x1, Pallas kernels, local(): pl.pallas_call(functools.partial(kernel, shape), out_shape=jax.ShapeDtype...  14 us
    unnamed x1, local copies, waits for them, and re-layouts  1.38 us

profile of v1, /device:TPU:0, one launch (start us, length us, event | category | flops | bytes accessed | tf_op | source)
XLA Modules:
  0.0 15.4 jit_solution(5034674558703070395)
XLA Ops:
  0.0 14.0 %shard_map.91 = bf16[16,1024]{1,0:T(8,128)(2,1)} custom-call(bf16[16,1024]{1,0:T(8,128)(2,1)} %rhs_h.1, bf16[4,64,256]{2,1,0:T(8,128)(2,1)} %basis_h.1, bf16[4,64,64]{2,1,0:T(8,128)(2,1)} %trans_h.1, bf16[4,6,64,64]{3,2,1,0:T(8,128)(2,1)} %coup_h.1, s32[4,6]{1,0:T(4,128)} %csrc_h.1, bf16[4,3,256,256]{3,2,1,0:T(8,128)(2,1)} %near_h.1, s32[4,3]{1,0:T(4,128)} %nsrc_h.1, ...), custom_call_target="tpu_custom_call" | custom-call | tf_op jit(solution)/shard_map/pallas_call | solution.py:299
  14.0 1.4 %copy.11 = bf16[16,1024]{1,0:T(8,128)(2,1)} copy(bf16[16,1024]{1,0:T(8,128)(2,1)} %shard_map.91) | data formatting | bytes 65536

commit v2 on v1

--- a/solution.py
+++ b/solution.py
@@ -31,8 +31,8 @@
     rhs_h, basis_h, trans_h, coup_h, csrc_h, near_h, nsrc_h, top_h, cc_h,
     out_ref,
     rhs_v, basis_v, trans_v, coup_v, csrc_s, near_v, nsrc_s, top_v, cc_v,
-    wide_x, wide_c, slots, part, part_in,
-    local_sem, halo_send, halo_recv, p_send, p_recv, r_send, r_recv,
+    wide_x, wide_c, slots,
+    local_sem, halo_send, halo_recv, p_send, p_recv,
 ):
     nx, ny, nz = shape
     count = nx * ny * nz
@@ -43,7 +43,7 @@
     topl = top_v.shape[0]
     gsize = 2**topl
     groups = count // gsize
-    blocks = part.shape[1] // rank
+    blocks = 2 if groups == 2 else 4
     width = blocks * rank
 
     me = (lax.axis_index("gx") * ny + lax.axis_index("gy")) * nz + lax.axis_index("gz")
@@ -67,15 +67,12 @@
     (l_rhs, l_basis, l_trans, l_top, l_cc, l_csrc, l_nsrc, l_coup, l_near) = loads
 
     if groups == 2:
-        across = (((me + gsize) % count, None, 0),)
+        mine = group
+        across = ((1 - group, None, 1 - group, group),)
     else:
-        across = ((me - gsize, group > 0, 1), (me + gsize, group < groups - 1, 0))
+        mine = 1
+        across = ((group - 1, group > 0, 0, 2), (group + 1, group < groups - 1, 2, 0))
     has_prev, has_next = me > 0, me < count - 1
-
-    barrier = pltpu.get_barrier_semaphore()
-
-    def greet(e):
-        pl.semaphore_signal(barrier, inc=1, device_id=place(e), device_id_type=MESH)
 
     def when(cond, fn):
         if cond is None:
@@ -83,18 +80,27 @@
         else:
             pl.when(cond)(fn)
 
-    peers = [group * gsize + (rel + r) % gsize for r in range(1, gsize)]
-    for e in peers:
-        greet(e)
+    far_first = sorted(range(gsize), key=lambda r: -(r % nz))
+
+    def each_peer(fn):
+        for i, (g, ok, _, there) in enumerate(across):
+            def outer(i=i, g=g, there=there):
+                for r in far_first:
+                    fn(g * gsize + (rel ^ r), there, i + 1)
+            when(ok, outer)
+        for r in far_first:
+            if r:
+                fn(group * gsize + (rel ^ r), mine, 0)
+
+    barrier = pltpu.get_barrier_semaphore()
+    each_peer(
+        lambda e, there, i: pl.semaphore_signal(
+            barrier, inc=1, device_id=place(e), device_id_type=MESH
+        )
+    )
     expected = jnp.int32(gsize - 1)
-    out_prev = has_prev & (rel == 0)
-    out_next = has_next & (rel == gsize - 1)
-    for e, ok, _ in across:
-        when(ok, functools.partial(greet, e))
-        expected += 1 if ok is None else ok.astype(jnp.int32)
-    for e, ok in ((me - 1, out_prev), (me + 1, out_next)):
-        when(ok, functools.partial(greet, e))
-        expected += ok.astype(jnp.int32)
+    for _, ok, _, _ in across:
+        expected += gsize if ok is None else gsize * ok.astype(jnp.int32)
 
     wide_x[leaves + 2 * REACH] = jnp.zeros((rows, leaf), BF16)
     wide_c[leaves + 2 * REACH] = jnp.zeros((rows, 2 * rank), BF16)
@@ -113,18 +119,17 @@
     pairs = [jnp.where(low, coeffs[t], coeffs[t + 1]) for t in range(0, leaves, 2)]
     l_trans.wait()
     root = mm(jnp.concatenate(pairs, 1), trans_v[...].reshape(leaves * rank, rank)).astype(BF16)
-    slots[rel] = jnp.concatenate([root, root], 1)
+    slots[mine, rel] = jnp.concatenate([root, root], 1)
 
     pl.semaphore_wait(barrier, expected)
 
-    sends = []
-    for e in peers:
-        copy = pltpu.make_async_remote_copy(
-            src_ref=slots.at[rel], dst_ref=slots.at[rel],
-            send_sem=p_send.at[0], recv_sem=p_recv.at[0],
+    each_peer(
+        lambda e, there, i: pltpu.make_async_remote_copy(
+            src_ref=slots.at[mine, rel], dst_ref=slots.at[there, rel],
+            send_sem=p_send.at[i], recv_sem=p_recv.at[there],
             device_id=place(e), device_id_type=MESH,
-        )
-        copy.start()
+        ).start()
+    )
 
     def halo(buf, i, up):
         first, land = (leaves, 0) if up else (REACH, leaves + REACH)
@@ -151,10 +156,9 @@
     l_cc.wait()
     lane_block = lax.broadcasted_iota(jnp.int32, (1, width), 1) // rank
     if groups == 2:
-        dest = jnp.where(lane_block == 0, me, (me + gsize) % count)
+        lane_group = lane_block
     else:
-        dest = jnp.where(lane_block == 0, me, jnp.where(lane_block == 1, me - gsize, me + gsize))
-        dest = jnp.where(lane_block == 3, -8 * gsize, dest)
+        lane_group = jnp.where(lane_block < 3, group - 1 + lane_block, -8)
     row = lax.broadcasted_iota(jnp.int32, (rank, rank), 0)
     col = lax.broadcasted_iota(jnp.int32, (rank, rank), 1)
     down = jnp.where(row == col, 1.0, 0.0).astype(BF16)
@@ -168,20 +172,20 @@
             mm_nt(cc_v[h].reshape(2 * rank, rank), jnp.concatenate([down] * blocks, 0))
         )
 
-    def coupled(h, cluster):
-        home = dest >> h
+    def coupled(h, c):
+        cluster = lane_group * 2 ** (topl - h) + c
+        home = me // 2**h
         return jnp.where(cluster == home - 1, reach_mats[h][:rank], 0.0) + jnp.where(
             cluster == home + 1, reach_mats[h][rank:], 0.0
         )
 
-    level = [coupled(topl, group)]
+    level = [coupled(topl, 0)]
     for h in range(topl - 1, -1, -1):
         wide = jnp.concatenate([m.astype(BF16) for m in level], 1)
         grown = mm(top_v[h].reshape(2 * rank, rank), wide)
-        first = group * 2 ** (topl - h)
         level = [
             grown[(c % 2) * rank:(c % 2 + 1) * rank, (c // 2) * width:(c // 2 + 1) * width]
-            + coupled(h, first + c)
+            + coupled(h, c)
             for c in range(2 ** (topl - h))
         ]
     gather_mat = jnp.concatenate([m.astype(BF16) for m in level], 0)
@@ -189,25 +193,6 @@
     spread = [mm_tn(trans_v[t], basis_v[t]).astype(BF16) for t in range(leaves)]
     spread = jnp.concatenate(spread, 1)
     spread = jnp.concatenate([spread] * blocks, 0)
-
-    everyone = pltpu.make_async_copy(
-        slots.at[pl.ds(0, gsize - 1)], slots.at[pl.ds(0, gsize - 1)], p_recv.at[0]
-    )
-    everyone.wait()
-    held = [jnp.where(low, slots[c], slots[c + 1]) for c in range(0, gsize, 2)]
-    own = mm(jnp.concatenate(held, 1), gather_mat)
-    part[...] = own
-
-    def partner(i, e, slot):
-        return pltpu.make_async_remote_copy(
-            src_ref=part, dst_ref=part_in.at[slot],
-            send_sem=r_send.at[i], recv_sem=r_recv.at[slot],
-            device_id=place(e), device_id_type=MESH,
-        )
-
-    partners = [(partner(i, e, slot), ok) for i, (e, ok, slot) in enumerate(across)]
-    for copy, ok in partners:
-        when(ok, copy.start)
 
     l_csrc.wait()
     l_nsrc.wait()
@@ -244,30 +229,37 @@
             + mm(field, basis_v[t])
         )
 
+    def landed(block, number, sem):
+        group_slots = slots.at[block, pl.ds(0, number)]
+        pltpu.make_async_copy(group_slots, group_slots, sem).wait()
+
+    landed(mine, gsize - 1, p_recv.at[mine])
+    for _, ok, here, _ in across:
+        when(ok, functools.partial(landed, here, gsize, p_recv.at[here]))
+    used = 2 if groups == 2 else 3
+    held = [
+        jnp.concatenate(
+            [jnp.where(low, slots[b, c], slots[b, c + 1]) for c in range(0, gsize, 2)], 1
+        )
+        for b in range(used)
+    ]
+    fields = mm(jnp.concatenate(held, 0), gather_mat)
     cells = lax.broadcasted_iota(jnp.int32, (rows, width), 1) // rank
-    if groups == 2:
-        partners[0][0].wait_recv()
-        total = jnp.where(cells == 0, own, part_in[0])
-    else:
-        def arrived(slot, ok):
-            pltpu.make_async_copy(part_in.at[slot], part_in.at[slot], r_recv.at[slot]).wait()
-
-        pl.when(group > 0)(functools.partial(arrived, 0, None))
-        pl.when(group < groups - 1)(functools.partial(arrived, 1, None))
-        total = jnp.where(cells == 0, own, 0.0)
-        total = jnp.where((cells == 1) & (group < groups - 1), part_in[1], total)
-        total = jnp.where((cells == 2) & (group > 0), part_in[0], total)
+    total = jnp.zeros((rows, width), F32)
+    for b in range(used):
+        ours = cells == b
+        if groups != 2 and b != 1:
+            ours = ours & (group > 0 if b == 0 else group < groups - 1)
+        total = jnp.where(ours, fields[b * rows:(b + 1) * rows], total)
     far = mm(total.astype(BF16), spread)
     for t in range(leaves):
         out_ref[:, t * leaf:(t + 1) * leaf] = (
             sums[t] + far[:, t * leaf:(t + 1) * leaf]
         ).astype(BF16)
 
-    pltpu.make_async_copy(
-        slots.at[pl.ds(0, gsize - 1)], slots.at[pl.ds(0, gsize - 1)], p_send.at[0]
-    ).wait()
-    for copy, ok in partners:
-        when(ok, copy.wait_send)
+    landed(mine, gsize - 1, p_send.at[0])
+    for i, (_, ok, here, _) in enumerate(across):
+        when(ok, functools.partial(landed, here, gsize, p_send.at[i + 1]))
 
     @pl.when(has_next)
     def _():
@@ -298,20 +290,17 @@
         dma = pltpu.SemaphoreType.DMA
         return pl.pallas_call(
             functools.partial(kernel, shape),
-            out_shape=jax.ShapeDtypeStruct(rhs.shape, BF16),
+            out_shape=pltpu.VMEM(rhs.shape, BF16),
             in_specs=[pl.BlockSpec(memory_space=pl.ANY)] * len(args),
             out_specs=pl.BlockSpec(memory_space=pltpu.VMEM),
             scratch_shapes=[room(x) for x in args] + [
                 pltpu.VMEM((leaves + 2 * REACH + 1, rows, leaf), BF16),
                 pltpu.VMEM((leaves + 2 * REACH + 1, rows, 2 * rank), BF16),
-                pltpu.VMEM((gsize, rows, 2 * rank), BF16),
-                pltpu.VMEM((rows, blocks * rank), F32),
-                pltpu.VMEM((blocks // 2, rows, blocks * rank), F32),
-                dma((len(args),)), dma((4,)), dma((4,)), dma((1,)), dma((1,)),
-                dma((2,)), dma((2,)),
+                pltpu.VMEM((blocks, gsize, rows, 2 * rank), BF16),
+                dma((len(args),)), dma((4,)), dma((4,)), dma((3,)), dma((blocks,)),
             ],
             compiler_params=pltpu.CompilerParams(collective_id=0, has_side_effects=True),
-        )(*args)
+        )(*(pltpu.with_memory_space_constraint(x, pltpu.HBM) for x in args))
 
     placed = (
         P(None, AXES),

time: 15.6 us -> 13.4 us (0.86)
  Pallas kernels: 14 us -> 12.6 us
  local copies, waits for them, and re-layouts: 1.38 us -> 0.62 us
    pallas_call x1, Pallas kernels: 14 us -> 12.6 us  [local(): pl.pallas_call(functools.partial(kernel, shape), out_shape=pltpu.VMEM(rhs...]
    unnamed x1, local copies, waits for them, and re-layouts: 1.38 us -> 0.62 us
where the time goes in v2:
time: 13.4 us; the launch traced here: 13.2 us
  Pallas kernels  12.6 us (94%)
  local copies, waits for them, and re-layouts  0.62 us (5%)
    pallas_call x1, Pallas kernels, local(): pl.pallas_call(functools.partial(kernel, shape), out_shape=pltpu.VMEM(rhs...  12.6 us
    unnamed x1, local copies, waits for them, and re-layouts  0.62 us

profile of v2, /device:TPU:0, one launch (start us, length us, event | category | flops | bytes accessed | tf_op | source)
XLA Modules:
  0.0 13.2 jit_solution(7378237838460741097)
XLA Ops:
  0.0 12.6 %shard_map.91 = bf16[16,1024]{1,0:T(8,128)(2,1)S(1)} custom-call(bf16[16,1024]{1,0:T(8,128)(2,1)} %rhs_h.1, bf16[4,64,256]{2,1,0:T(8,128)(2,1)} %basis_h.1, bf16[4,64,64]{2,1,0:T(8,128)(2,1)} %trans_h.1, bf16[4,6,64,64]{3,2,1,0:T(8,128)(2,1)} %coup_h.1, s32[4,6]{1,0:T(4,128)} %csrc_h.1, bf16[4,3,256,256]{3,2,1,0:T(8,128)(2,1)} %near_h.1, s32[4,3]{1,0:T(4,128)} %nsrc_h.1, ...), custom_call_target="tpu_custom_call" | custom-call | tf_op jit(solution)/shard_map/pallas_call | solution.py:291
  12.6 0.6 %copy.11 = bf16[16,1024]{1,0:T(8,128)(2,1)} copy(bf16[16,1024]{1,0:T(8,128)(2,1)S(1)} %shard_map.91) | data formatting | bytes 65536

commit v3 on v2

--- a/solution.py
+++ b/solution.py
@@ -9,6 +9,7 @@
 
 AXES = ("gx", "gy", "gz")
 REACH = 2
+LOW = 2
 MESH = pl.DeviceIdType.MESH
 BF16 = jnp.bfloat16
 F32 = jnp.float32
@@ -31,8 +32,8 @@
     rhs_h, basis_h, trans_h, coup_h, csrc_h, near_h, nsrc_h, top_h, cc_h,
     out_ref,
     rhs_v, basis_v, trans_v, coup_v, csrc_s, near_v, nsrc_s, top_v, cc_v,
-    wide_x, wide_c, slots,
-    local_sem, halo_send, halo_recv, p_send, p_recv,
+    wide_x, wide_c, slots, part, part_in,
+    local_sem, halo_send, halo_recv, p_send, p_recv, r_send, r_recv,
 ):
     nx, ny, nz = shape
     count = nx * ny * nz
@@ -43,12 +44,15 @@
     topl = top_v.shape[0]
     gsize = 2**topl
     groups = count // gsize
-    blocks = 2 if groups == 2 else 4
-    width = blocks * rank
+    line = 2**LOW
+    lines = gsize // line
+    width = part.shape[0] * 2 * rank
 
     me = (lax.axis_index("gx") * ny + lax.axis_index("gy")) * nz + lax.axis_index("gz")
     group = me // gsize
-    rel = me % gsize
+    mine_line = me // line
+    rel = me % line
+    own = mine_line % lines
 
     def place(e):
         return (e // (ny * nz), (e // nz) % ny, e % nz)
@@ -80,27 +84,35 @@
         else:
             pl.when(cond)(fn)
 
-    far_first = sorted(range(gsize), key=lambda r: -(r % nz))
-
-    def each_peer(fn):
-        for i, (g, ok, _, there) in enumerate(across):
-            def outer(i=i, g=g, there=there):
-                for r in far_first:
-                    fn(g * gsize + (rel ^ r), there, i + 1)
+    mates = [mine_line * line + (rel ^ r) for r in range(line - 1, 0, -1)]
+
+    def each_line(fn):
+        for i, (g, ok, here, there) in enumerate(across):
+            def outer(i=i, g=g, here=here, there=there):
+                for k in range(lines):
+                    l = own ^ k
+                    fn(g * gsize + l * line + rel, here, l, there, i + 1)
             when(ok, outer)
-        for r in far_first:
-            if r:
-                fn(group * gsize + (rel ^ r), mine, 0)
+        for k in range(lines - 1, 0, -1):
+            l = own ^ k
+            fn(group * gsize + l * line + rel, mine, l, mine, 0)
 
     barrier = pltpu.get_barrier_semaphore()
-    each_peer(
-        lambda e, there, i: pl.semaphore_signal(
-            barrier, inc=1, device_id=place(e), device_id_type=MESH
-        )
-    )
-    expected = jnp.int32(gsize - 1)
+
+    def greet(e, *_):
+        pl.semaphore_signal(barrier, inc=1, device_id=place(e), device_id_type=MESH)
+
+    for e in mates:
+        greet(e)
+    out_prev = has_prev & (rel == 0)
+    out_next = has_next & (rel == line - 1)
+    when(out_prev, functools.partial(greet, me - 1))
+    when(out_next, functools.partial(greet, me + 1))
+    each_line(greet)
+    expected = jnp.int32(line - 1 + lines - 1)
+    expected += out_prev.astype(jnp.int32) + out_next.astype(jnp.int32)
     for _, ok, _, _ in across:
-        expected += gsize if ok is None else gsize * ok.astype(jnp.int32)
+        expected += lines if ok is None else lines * ok.astype(jnp.int32)
 
     wide_x[leaves + 2 * REACH] = jnp.zeros((rows, leaf), BF16)
     wide_c[leaves + 2 * REACH] = jnp.zeros((rows, 2 * rank), BF16)
@@ -119,17 +131,16 @@
     pairs = [jnp.where(low, coeffs[t], coeffs[t + 1]) for t in range(0, leaves, 2)]
     l_trans.wait()
     root = mm(jnp.concatenate(pairs, 1), trans_v[...].reshape(leaves * rank, rank)).astype(BF16)
-    slots[mine, rel] = jnp.concatenate([root, root], 1)
+    slots[rel] = jnp.concatenate([root, root], 1)
 
     pl.semaphore_wait(barrier, expected)
 
-    each_peer(
-        lambda e, there, i: pltpu.make_async_remote_copy(
-            src_ref=slots.at[mine, rel], dst_ref=slots.at[there, rel],
-            send_sem=p_send.at[i], recv_sem=p_recv.at[there],
+    for e in mates:
+        pltpu.make_async_remote_copy(
+            src_ref=slots.at[rel], dst_ref=slots.at[rel],
+            send_sem=p_send.at[0], recv_sem=p_recv.at[0],
             device_id=place(e), device_id_type=MESH,
         ).start()
-    )
 
     def halo(buf, i, up):
         first, land = (leaves, 0) if up else (REACH, leaves + REACH)
@@ -155,10 +166,10 @@
     l_top.wait()
     l_cc.wait()
     lane_block = lax.broadcasted_iota(jnp.int32, (1, width), 1) // rank
-    if groups == 2:
-        lane_group = lane_block
-    else:
-        lane_group = jnp.where(lane_block < 3, group - 1 + lane_block, -8)
+    lane_group = lane_block // lines
+    if groups != 2:
+        lane_group = lane_group + (group - 1)
+    dest = lane_group * gsize + (lane_block % lines) * line + rel
     row = lax.broadcasted_iota(jnp.int32, (rank, rank), 0)
     col = lax.broadcasted_iota(jnp.int32, (rank, rank), 1)
     down = jnp.where(row == col, 1.0, 0.0).astype(BF16)
@@ -166,33 +177,55 @@
     for h in range(topl + 1):
         if h == 1:
             down = top_v[0, rel % 2]
-        elif h > 1:
+        elif 1 < h <= LOW:
             down = mm(down, top_v[h - 1, (rel // 2 ** (h - 1)) % 2]).astype(BF16)
-        reach_mats.append(
-            mm_nt(cc_v[h].reshape(2 * rank, rank), jnp.concatenate([down] * blocks, 0))
-        )
-
-    def coupled(h, c):
-        cluster = lane_group * 2 ** (topl - h) + c
-        home = me // 2**h
+        elif h > LOW:
+            down = jnp.concatenate([mm(down, top_v[h - 1, p]) for p in range(2)], 0).astype(BF16)
+        stack = down if h > LOW else jnp.concatenate([down, down], 0)
+        mat = mm_nt(cc_v[h].reshape(2 * rank, rank), stack)
+        reach_mats.append(jnp.concatenate([mat] * (width // mat.shape[1]), 1))
+
+    def coupled(h, cluster):
+        home = dest >> h
         return jnp.where(cluster == home - 1, reach_mats[h][:rank], 0.0) + jnp.where(
             cluster == home + 1, reach_mats[h][rank:], 0.0
         )
 
-    level = [coupled(topl, 0)]
+    level = [coupled(topl, group)]
     for h in range(topl - 1, -1, -1):
         wide = jnp.concatenate([m.astype(BF16) for m in level], 1)
+        if h >= LOW:
+            level = [mm(top_v[h, (me >> h) % 2], wide) + coupled(h, me >> h)]
+            continue
         grown = mm(top_v[h].reshape(2 * rank, rank), wide)
         level = [
             grown[(c % 2) * rank:(c % 2 + 1) * rank, (c // 2) * width:(c // 2 + 1) * width]
-            + coupled(h, c)
-            for c in range(2 ** (topl - h))
+            + coupled(h, mine_line * 2 ** (LOW - h) + c)
+            for c in range(2 ** (LOW - h))
         ]
     gather_mat = jnp.concatenate([m.astype(BF16) for m in level], 0)
 
     spread = [mm_tn(trans_v[t], basis_v[t]).astype(BF16) for t in range(leaves)]
     spread = jnp.concatenate(spread, 1)
-    spread = jnp.concatenate([spread] * blocks, 0)
+    spread = jnp.concatenate([spread, spread], 0)
+
+    def landed(buf, number, sem):
+        some = buf.at[pl.ds(0, number)]
+        pltpu.make_async_copy(some, some, sem).wait()
+
+    landed(slots, line - 1, p_recv.at[0])
+    held = [jnp.where(low, slots[c], slots[c + 1]) for c in range(0, line, 2)]
+    parts = mm(jnp.concatenate(held, 1), gather_mat)
+    for i in range(part.shape[0]):
+        part[i] = parts[:, i * 2 * rank:(i + 1) * 2 * rank]
+    each_line(
+        lambda e, here, l, there, i: pltpu.make_async_remote_copy(
+            src_ref=part.at[here * (lines // 2) + l // 2], dst_ref=part_in.at[there * lines + own],
+            send_sem=r_send.at[i], recv_sem=r_recv.at[there],
+            device_id=place(e), device_id_type=MESH,
+        ).start()
+    )
+    part_in[mine * lines + own] = part[mine * (lines // 2) + own // 2]
 
     l_csrc.wait()
     l_nsrc.wait()
@@ -229,37 +262,26 @@
             + mm(field, basis_v[t])
         )
 
-    def landed(block, number, sem):
-        group_slots = slots.at[block, pl.ds(0, number)]
-        pltpu.make_async_copy(group_slots, group_slots, sem).wait()
-
-    landed(mine, gsize - 1, p_recv.at[mine])
+    landed(part_in, lines - 1, r_recv.at[mine])
     for _, ok, here, _ in across:
-        when(ok, functools.partial(landed, here, gsize, p_recv.at[here]))
-    used = 2 if groups == 2 else 3
-    held = [
-        jnp.concatenate(
-            [jnp.where(low, slots[b, c], slots[b, c + 1]) for c in range(0, gsize, 2)], 1
-        )
-        for b in range(used)
-    ]
-    fields = mm(jnp.concatenate(held, 0), gather_mat)
-    cells = lax.broadcasted_iota(jnp.int32, (rows, width), 1) // rank
-    total = jnp.zeros((rows, width), F32)
-    for b in range(used):
-        ours = cells == b
-        if groups != 2 and b != 1:
-            ours = ours & (group > 0 if b == 0 else group < groups - 1)
-        total = jnp.where(ours, fields[b * rows:(b + 1) * rows], total)
+        when(ok, functools.partial(landed, part_in, lines, r_recv.at[here]))
+    total = jnp.zeros((rows, 2 * rank), F32)
+    for j in range(part_in.shape[0]):
+        term = part_in[j]
+        if groups != 2 and j // lines != 1:
+            term = jnp.where(group > 0 if j < lines else group < groups - 1, term, 0.0)
+        total += term
+    total = jnp.where(low == (own % 2 == 0), total, 0.0)
     far = mm(total.astype(BF16), spread)
     for t in range(leaves):
         out_ref[:, t * leaf:(t + 1) * leaf] = (
             sums[t] + far[:, t * leaf:(t + 1) * leaf]
         ).astype(BF16)
 
-    landed(mine, gsize - 1, p_send.at[0])
-    for i, (_, ok, here, _) in enumerate(across):
-        when(ok, functools.partial(landed, here, gsize, p_send.at[i + 1]))
+    landed(slots, line - 1, p_send.at[0])
+    landed(part_in, lines - 1, r_send.at[0])
+    for i, (_, ok, _, _) in enumerate(across):
+        when(ok, functools.partial(landed, part_in, lines, r_send.at[i + 1]))
 
     @pl.when(has_next)
     def _():
@@ -280,7 +302,7 @@
         leaves, rank, leaf = basis.shape
         rows = rhs.shape[0]
         gsize = 2 ** top.shape[0]
-        blocks = 2 if count == 2 * gsize else 4
+        lines = (2 if count == 2 * gsize else 3) * gsize // 2**LOW
         args = (rhs, basis, trans, coup, csrc, near, nsrc, top, cc)
 
         def room(x):
@@ -296,8 +318,11 @@
             scratch_shapes=[room(x) for x in args] + [
                 pltpu.VMEM((leaves + 2 * REACH + 1, rows, leaf), BF16),
                 pltpu.VMEM((leaves + 2 * REACH + 1, rows, 2 * rank), BF16),
-                pltpu.VMEM((blocks, gsize, rows, 2 * rank), BF16),
-                dma((len(args),)), dma((4,)), dma((4,)), dma((3,)), dma((blocks,)),
+                pltpu.VMEM((2**LOW, rows, 2 * rank), BF16),
+                pltpu.VMEM((lines // 2, rows, 2 * rank), F32),
+                pltpu.VMEM((lines, rows, 2 * rank), F32),
+                dma((len(args),)), dma((4,)), dma((4,)), dma((1,)), dma((1,)),
+                dma((3,)), dma((3,)),
             ],
             compiler_params=pltpu.CompilerParams(collective_id=0, has_side_effects=True),
         )(*(pltpu.with_memory_space_constraint(x, pltpu.HBM) for x in args))

time: 13.4 us -> 13.5 us (level)
  no operation moved by 1% of the time
where the time goes in v3:
time: 13.5 us; the launch traced here: 13.3 us
  Pallas kernels  12.7 us (94%)
  local copies, waits for them, and re-layouts  0.62 us (5%)
    pallas_call x1, Pallas kernels, local(): pl.pallas_call(functools.partial(kernel, shape), out_shape=pltpu.VMEM(rhs...  12.7 us
    unnamed x1, local copies, waits for them, and re-layouts  0.62 us

profile of v3, /device:TPU:0, one launch (start us, length us, event | category | flops | bytes accessed | tf_op | source)
XLA Modules:
  0.0 13.3 jit_solution(10203529999892579757)
XLA Ops:
  0.0 12.7 %shard_map.91 = bf16[16,1024]{1,0:T(8,128)(2,1)S(1)} custom-call(bf16[16,1024]{1,0:T(8,128)(2,1)} %rhs_h.1, bf16[4,64,256]{2,1,0:T(8,128)(2,1)} %basis_h.1, bf16[4,64,64]{2,1,0:T(8,128)(2,1)} %trans_h.1, bf16[4,6,64,64]{3,2,1,0:T(8,128)(2,1)} %coup_h.1, s32[4,6]{1,0:T(4,128)} %csrc_h.1, bf16[4,3,256,256]{3,2,1,0:T(8,128)(2,1)} %near_h.1, s32[4,3]{1,0:T(4,128)} %nsrc_h.1, ...), custom_call_target="tpu_custom_call" | custom-call | tf_op jit(solution)/shard_map/pallas_call | solution.py:313
  12.7 0.6 %copy.11 = bf16[16,1024]{1,0:T(8,128)(2,1)} copy(bf16[16,1024]{1,0:T(8,128)(2,1)S(1)} %shard_map.91) | data formatting | bytes 65536

commit v4 on v3

--- a/solution.py
+++ b/solution.py
@@ -32,7 +32,7 @@
     rhs_h, basis_h, trans_h, coup_h, csrc_h, near_h, nsrc_h, top_h, cc_h,
     out_ref,
     rhs_v, basis_v, trans_v, coup_v, csrc_s, near_v, nsrc_s, top_v, cc_v,
-    wide_x, wide_c, slots, part, part_in,
+    wide_x, wide_c, slots, part, part_in, gather_v, spread_v, first_v,
     local_sem, halo_send, halo_recv, p_send, p_recv, r_send, r_recv,
 ):
     nx, ny, nz = shape
@@ -133,15 +133,6 @@
     root = mm(jnp.concatenate(pairs, 1), trans_v[...].reshape(leaves * rank, rank)).astype(BF16)
     slots[rel] = jnp.concatenate([root, root], 1)
 
-    pl.semaphore_wait(barrier, expected)
-
-    for e in mates:
-        pltpu.make_async_remote_copy(
-            src_ref=slots.at[rel], dst_ref=slots.at[rel],
-            send_sem=p_send.at[0], recv_sem=p_recv.at[0],
-            device_id=place(e), device_id_type=MESH,
-        ).start()
-
     def halo(buf, i, up):
         first, land = (leaves, 0) if up else (REACH, leaves + REACH)
         return pltpu.make_async_remote_copy(
@@ -153,61 +144,85 @@
     ups = (halo(wide_c, 0, True), halo(wide_x, 1, True))
     downs = (halo(wide_c, 2, False), halo(wide_x, 3, False))
 
-    @pl.when(has_next)
-    def _():
-        for copy in ups:
-            copy.start()
-
-    @pl.when(has_prev)
-    def _():
-        for copy in downs:
-            copy.start()
-
-    l_top.wait()
-    l_cc.wait()
-    lane_block = lax.broadcasted_iota(jnp.int32, (1, width), 1) // rank
-    lane_group = lane_block // lines
-    if groups != 2:
-        lane_group = lane_group + (group - 1)
-    dest = lane_group * gsize + (lane_block % lines) * line + rel
-    row = lax.broadcasted_iota(jnp.int32, (rank, rank), 0)
-    col = lax.broadcasted_iota(jnp.int32, (rank, rank), 1)
-    down = jnp.where(row == col, 1.0, 0.0).astype(BF16)
-    reach_mats = []
-    for h in range(topl + 1):
-        if h == 1:
-            down = top_v[0, rel % 2]
-        elif 1 < h <= LOW:
-            down = mm(down, top_v[h - 1, (rel // 2 ** (h - 1)) % 2]).astype(BF16)
-        elif h > LOW:
-            down = jnp.concatenate([mm(down, top_v[h - 1, p]) for p in range(2)], 0).astype(BF16)
-        stack = down if h > LOW else jnp.concatenate([down, down], 0)
-        mat = mm_nt(cc_v[h].reshape(2 * rank, rank), stack)
-        reach_mats.append(jnp.concatenate([mat] * (width // mat.shape[1]), 1))
-
-    def coupled(h, cluster):
-        home = dest >> h
-        return jnp.where(cluster == home - 1, reach_mats[h][:rank], 0.0) + jnp.where(
-            cluster == home + 1, reach_mats[h][rank:], 0.0
-        )
-
-    level = [coupled(topl, group)]
-    for h in range(topl - 1, -1, -1):
-        wide = jnp.concatenate([m.astype(BF16) for m in level], 1)
-        if h >= LOW:
-            level = [mm(top_v[h, (me >> h) % 2], wide) + coupled(h, me >> h)]
-            continue
-        grown = mm(top_v[h].reshape(2 * rank, rank), wide)
-        level = [
-            grown[(c % 2) * rank:(c % 2 + 1) * rank, (c // 2) * width:(c // 2 + 1) * width]
-            + coupled(h, mine_line * 2 ** (LOW - h) + c)
-            for c in range(2 ** (LOW - h))
-        ]
-    gather_mat = jnp.concatenate([m.astype(BF16) for m in level], 0)
-
-    spread = [mm_tn(trans_v[t], basis_v[t]).astype(BF16) for t in range(leaves)]
-    spread = jnp.concatenate(spread, 1)
-    spread = jnp.concatenate([spread, spread], 0)
+    def send():
+        pl.semaphore_wait(barrier, expected)
+
+        for e in mates:
+            pltpu.make_async_remote_copy(
+                src_ref=slots.at[rel], dst_ref=slots.at[rel],
+                send_sem=p_send.at[0], recv_sem=p_recv.at[0],
+                device_id=place(e), device_id_type=MESH,
+            ).start()
+        @pl.when(has_next)
+        def _():
+            for copy in ups:
+                copy.start()
+
+        @pl.when(has_prev)
+        def _():
+            for copy in downs:
+                copy.start()
+
+    def prepare():
+        l_top.wait()
+        l_cc.wait()
+        lane_block = lax.broadcasted_iota(jnp.int32, (1, width), 1) // rank
+        lane_group = lane_block // lines
+        if groups != 2:
+            lane_group = lane_group + (group - 1)
+        dest = lane_group * gsize + (lane_block % lines) * line + rel
+        row = lax.broadcasted_iota(jnp.int32, (rank, rank), 0)
+        col = lax.broadcasted_iota(jnp.int32, (rank, rank), 1)
+        down = jnp.where(row == col, 1.0, 0.0).astype(BF16)
+        reach_mats = []
+        for h in range(topl + 1):
+            if h == 1:
+                down = top_v[0, rel % 2]
+            elif 1 < h <= LOW:
+                down = mm(down, top_v[h - 1, (rel // 2 ** (h - 1)) % 2]).astype(BF16)
+            elif h > LOW:
+                down = jnp.concatenate([mm(down, top_v[h - 1, p]) for p in range(2)], 0).astype(BF16)
+            stack = down if h > LOW else jnp.concatenate([down, down], 0)
+            mat = mm_nt(cc_v[h].reshape(2 * rank, rank), stack)
+            reach_mats.append(jnp.concatenate([mat] * (width // mat.shape[1]), 1))
+
+        def coupled(h, cluster):
+            home = dest >> h
+            return jnp.where(cluster == home - 1, reach_mats[h][:rank], 0.0) + jnp.where(
+                cluster == home + 1, reach_mats[h][rank:], 0.0
+            )
+
+        level = [coupled(topl, group)]
+        for h in range(topl - 1, -1, -1):
+            wide = jnp.concatenate([m.astype(BF16) for m in level], 1)
+            if h >= LOW:
+                level = [mm(top_v[h, (me >> h) % 2], wide) + coupled(h, me >> h)]
+                continue
+            grown = mm(top_v[h].reshape(2 * rank, rank), wide)
+            level = [
+                grown[(c % 2) * rank:(c % 2 + 1) * rank, (c // 2) * width:(c // 2 + 1) * width]
+                + coupled(h, mine_line * 2 ** (LOW - h) + c)
+                for c in range(2 ** (LOW - h))
+            ]
+        for c, m in enumerate(level):
+            gather_v[c * rank:(c + 1) * rank] = m.astype(BF16)
+
+        for t in range(leaves):
+            mat = mm_tn(trans_v[t], basis_v[t]).astype(BF16)
+            spread_v[:rank, t * leaf:(t + 1) * leaf] = mat
+            spread_v[rank:, t * leaf:(t + 1) * leaf] = mat
+        l_near.wait()
+        for t in range(leaves):
+            first_v[:, t * leaf:(t + 1) * leaf] = mm(wide_x[REACH + t], near_v[t, 0])
+
+    turn = jnp.where(rel < line // 2, 0, 1)
+
+    def step(i, carry):
+        pl.when(i == turn)(prepare)
+        pl.when(i != turn)(send)
+        return carry
+
+    lax.fori_loop(0, 2, step, 0)
 
     def landed(buf, number, sem):
         some = buf.at[pl.ds(0, number)]
@@ -215,7 +230,7 @@
 
     landed(slots, line - 1, p_recv.at[0])
     held = [jnp.where(low, slots[c], slots[c + 1]) for c in range(0, line, 2)]
-    parts = mm(jnp.concatenate(held, 1), gather_mat)
+    parts = mm(jnp.concatenate(held, 1), gather_v[...])
     for i in range(part.shape[0]):
         part[i] = parts[:, i * 2 * rank:(i + 1) * 2 * rank]
     each_line(
@@ -230,7 +245,6 @@
     l_csrc.wait()
     l_nsrc.wait()
     l_coup.wait()
-    l_near.wait()
 
     @pl.when(has_prev)
     def _():
@@ -255,10 +269,10 @@
         field = mm(
             jnp.concatenate(picked, 1), coup_v[t].reshape(slots_adm * rank, rank)
         ).astype(BF16)
-        inputs = [wide_x[REACH + t]]
-        inputs += [wide_x[spot(nsrc_s[t, n])] for n in range(1, slots_near)]
+        inputs = [wide_x[spot(nsrc_s[t, n])] for n in range(1, slots_near)]
         sums.append(
-            mm(jnp.concatenate(inputs, 1), near_v[t].reshape(slots_near * leaf, leaf))
+            mm(jnp.concatenate(inputs, 1), near_v[t, 1:].reshape(-1, leaf))
+            + first_v[:, t * leaf:(t + 1) * leaf]
             + mm(field, basis_v[t])
         )
 
@@ -272,7 +286,7 @@
             term = jnp.where(group > 0 if j < lines else group < groups - 1, term, 0.0)
         total += term
     total = jnp.where(low == (own % 2 == 0), total, 0.0)
-    far = mm(total.astype(BF16), spread)
+    far = mm(total.astype(BF16), spread_v[...])
     for t in range(leaves):
         out_ref[:, t * leaf:(t + 1) * leaf] = (
             sums[t] + far[:, t * leaf:(t + 1) * leaf]
@@ -321,6 +335,9 @@
                 pltpu.VMEM((2**LOW, rows, 2 * rank), BF16),
                 pltpu.VMEM((lines // 2, rows, 2 * rank), F32),
                 pltpu.VMEM((lines, rows, 2 * rank), F32),
+                pltpu.VMEM((2**LOW * rank, lines * rank), BF16),
+                pltpu.VMEM((2 * rank, leaves * leaf), BF16),
+                pltpu.VMEM((rows, leaves * leaf), F32),
                 dma((len(args),)), dma((4,)), dma((4,)), dma((1,)), dma((1,)),
                 dma((3,)), dma((3,)),
             ],

time: 13.5 us -> 13.5 us (level)
  no operation moved by 1% of the time
where the time goes in v4:
time: 13.5 us; the launch traced here: 13.3 us
  Pallas kernels  12.7 us (94%)
  local copies, waits for them, and re-layouts  0.62 us (5%)
    pallas_call x1, Pallas kernels, local(): pl.pallas_call(functools.partial(kernel, shape), out_shape=pltpu.VMEM(rhs...  12.7 us
    unnamed x1, local copies, waits for them, and re-layouts  0.62 us

profile of v4, /device:TPU:0, one launch (start us, length us, event | category | flops | bytes accessed | tf_op | source)
XLA Modules:
  0.0 13.3 jit_solution(2337191365646909219)
XLA Ops:
  0.0 12.7 %shard_map.91 = bf16[16,1024]{1,0:T(8,128)(2,1)S(1)} custom-call(bf16[16,1024]{1,0:T(8,128)(2,1)} %rhs_h.1, bf16[4,64,256]{2,1,0:T(8,128)(2,1)} %basis_h.1, bf16[4,64,64]{2,1,0:T(8,128)(2,1)} %trans_h.1, bf16[4,6,64,64]{3,2,1,0:T(8,128)(2,1)} %coup_h.1, s32[4,6]{1,0:T(4,128)} %csrc_h.1, bf16[4,3,256,256]{3,2,1,0:T(8,128)(2,1)} %near_h.1, s32[4,3]{1,0:T(4,128)} %nsrc_h.1, ...), custom_call_target="tpu_custom_call" | custom-call | tf_op jit(solution)/shard_map/pallas_call | solution.py:327
  12.7 0.6 %copy.11 = bf16[16,1024]{1,0:T(8,128)(2,1)} copy(bf16[16,1024]{1,0:T(8,128)(2,1)S(1)} %shard_map.91) | data formatting | bytes 65536

commit v5 on v4

--- a/solution.py
+++ b/solution.py
@@ -114,8 +114,6 @@
     for _, ok, _, _ in across:
         expected += lines if ok is None else lines * ok.astype(jnp.int32)
 
-    wide_x[leaves + 2 * REACH] = jnp.zeros((rows, leaf), BF16)
-    wide_c[leaves + 2 * REACH] = jnp.zeros((rows, 2 * rank), BF16)
     low = lax.broadcasted_iota(jnp.int32, (rows, 2 * rank), 1) < rank
 
     l_rhs.wait()
@@ -123,15 +121,18 @@
     coeffs = []
     for t in range(leaves):
         block = rhs_v[:, t * leaf:(t + 1) * leaf]
-        wide_x[REACH + t] = block
         basis = basis_v[t]
         both = mm_nt(block, jnp.concatenate([basis, basis], 0)).astype(BF16)
-        wide_c[REACH + t] = both
         coeffs.append(both)
     pairs = [jnp.where(low, coeffs[t], coeffs[t + 1]) for t in range(0, leaves, 2)]
     l_trans.wait()
     root = mm(jnp.concatenate(pairs, 1), trans_v[...].reshape(leaves * rank, rank)).astype(BF16)
     slots[rel] = jnp.concatenate([root, root], 1)
+    for t in range(leaves):
+        wide_x[REACH + t] = rhs_v[:, t * leaf:(t + 1) * leaf]
+        wide_c[REACH + t] = coeffs[t]
+    wide_x[leaves + 2 * REACH] = jnp.zeros((rows, leaf), BF16)
+    wide_c[leaves + 2 * REACH] = jnp.zeros((rows, 2 * rank), BF16)
 
     def halo(buf, i, up):
         first, land = (leaves, 0) if up else (REACH, leaves + REACH)
@@ -224,6 +225,38 @@
 
     lax.fori_loop(0, 2, step, 0)
 
+    l_csrc.wait()
+    l_nsrc.wait()
+    l_coup.wait()
+
+    @pl.when(has_prev)
+    def _():
+        for copy in ups:
+            copy.wait_recv()
+
+    @pl.when(has_next)
+    def _():
+        for copy in downs:
+            copy.wait_recv()
+
+    anchor = me * leaves - REACH
+    last = leaves + 2 * REACH
+
+    def spot(source):
+        return jnp.where(source >= 0, jnp.clip(source - anchor, 0, last - 1), last)
+
+    for t in range(leaves):
+        picked = [wide_c[spot(csrc_s[t, a])] for a in range(slots_adm)]
+        picked = [jnp.where(low, picked[a], picked[a + 1]) for a in range(0, slots_adm, 2)]
+        field = mm(
+            jnp.concatenate(picked, 1), coup_v[t].reshape(slots_adm * rank, rank)
+        ).astype(BF16)
+        inputs = [wide_x[spot(nsrc_s[t, n])] for n in range(1, slots_near)]
+        first_v[:, t * leaf:(t + 1) * leaf] += (
+            mm(jnp.concatenate(inputs, 1), near_v[t, 1:].reshape(-1, leaf))
+            + mm(field, basis_v[t])
+        )
+
     def landed(buf, number, sem):
         some = buf.at[pl.ds(0, number)]
         pltpu.make_async_copy(some, some, sem).wait()
@@ -242,40 +275,6 @@
     )
     part_in[mine * lines + own] = part[mine * (lines // 2) + own // 2]
 
-    l_csrc.wait()
-    l_nsrc.wait()
-    l_coup.wait()
-
-    @pl.when(has_prev)
-    def _():
-        for copy in ups:
-            copy.wait_recv()
-
-    @pl.when(has_next)
-    def _():
-        for copy in downs:
-            copy.wait_recv()
-
-    anchor = me * leaves - REACH
-    last = leaves + 2 * REACH
-
-    def spot(source):
-        return jnp.where(source >= 0, jnp.clip(source - anchor, 0, last - 1), last)
-
-    sums = []
-    for t in range(leaves):
-        picked = [wide_c[spot(csrc_s[t, a])] for a in range(slots_adm)]
-        picked = [jnp.where(low, picked[a], picked[a + 1]) for a in range(0, slots_adm, 2)]
-        field = mm(
-            jnp.concatenate(picked, 1), coup_v[t].reshape(slots_adm * rank, rank)
-        ).astype(BF16)
-        inputs = [wide_x[spot(nsrc_s[t, n])] for n in range(1, slots_near)]
-        sums.append(
-            mm(jnp.concatenate(inputs, 1), near_v[t, 1:].reshape(-1, leaf))
-            + first_v[:, t * leaf:(t + 1) * leaf]
-            + mm(field, basis_v[t])
-        )
-
     landed(part_in, lines - 1, r_recv.at[mine])
     for _, ok, here, _ in across:
         when(ok, functools.partial(landed, part_in, lines, r_recv.at[here]))
@@ -289,7 +288,7 @@
     far = mm(total.astype(BF16), spread_v[...])
     for t in range(leaves):
         out_ref[:, t * leaf:(t + 1) * leaf] = (
-            sums[t] + far[:, t * leaf:(t + 1) * leaf]
+            first_v[:, t * leaf:(t + 1) * leaf] + far[:, t * leaf:(t + 1) * leaf]
         ).astype(BF16)
 
     landed(slots, line - 1, p_send.at[0])

time: 13.5 us -> 14.2 us (1.052)
  Pallas kernels: 12.7 us -> 13.5 us
    pallas_call x1, Pallas kernels: 12.7 us -> 13.5 us  [local(): pl.pallas_call(functools.partial(kernel, shape), out_shape=pltpu.VMEM(rhs...]
where the time goes in v5:
time: 14.2 us; the launch traced here: 14.1 us
  Pallas kernels  13.5 us (95%)
  local copies, waits for them, and re-layouts  0.62 us (4%)
    pallas_call x1, Pallas kernels, local(): pl.pallas_call(functools.partial(kernel, shape), out_shape=pltpu.VMEM(rhs...  13.5 us
    unnamed x1, local copies, waits for them, and re-layouts  0.62 us

profile of v5, /device:TPU:0, one launch (start us, length us, event | category | flops | bytes accessed | tf_op | source)
XLA Modules:
  0.0 14.1 jit_solution(5229989683321302084)
XLA Ops:
  0.0 13.5 %shard_map.91 = bf16[16,1024]{1,0:T(8,128)(2,1)S(1)} custom-call(bf16[16,1024]{1,0:T(8,128)(2,1)} %rhs_h.1, bf16[4,64,256]{2,1,0:T(8,128)(2,1)} %basis_h.1, bf16[4,64,64]{2,1,0:T(8,128)(2,1)} %trans_h.1, bf16[4,6,64,64]{3,2,1,0:T(8,128)(2,1)} %coup_h.1, s32[4,6]{1,0:T(4,128)} %csrc_h.1, bf16[4,3,256,256]{3,2,1,0:T(8,128)(2,1)} %near_h.1, s32[4,3]{1,0:T(4,128)} %nsrc_h.1, ...), custom_call_target="tpu_custom_call" | custom-call | tf_op jit(solution)/shard_map/pallas_call | solution.py:326
  13.5 0.6 %copy.11 = bf16[16,1024]{1,0:T(8,128)(2,1)} copy(bf16[16,1024]{1,0:T(8,128)(2,1)S(1)} %shard_map.91) | data formatting | bytes 65536

commit v6 on v2

--- a/solution.py
+++ b/solution.py
@@ -9,6 +9,7 @@
 
 AXES = ("gx", "gy", "gz")
 REACH = 2
+LOW = 2
 MESH = pl.DeviceIdType.MESH
 BF16 = jnp.bfloat16
 F32 = jnp.float32
@@ -31,7 +32,7 @@
     rhs_h, basis_h, trans_h, coup_h, csrc_h, near_h, nsrc_h, top_h, cc_h,
     out_ref,
     rhs_v, basis_v, trans_v, coup_v, csrc_s, near_v, nsrc_s, top_v, cc_v,
-    wide_x, wide_c, slots,
+    low_x, low_c, high_x, high_c, slots,
     local_sem, halo_send, halo_recv, p_send, p_recv,
 ):
     nx, ny, nz = shape
@@ -48,7 +49,10 @@
 
     me = (lax.axis_index("gx") * ny + lax.axis_index("gy")) * nz + lax.axis_index("gz")
     group = me // gsize
-    rel = me % gsize
+    line = 2**LOW
+    lines = gsize // line
+    own = me % gsize // line
+    pos = me % line
 
     def place(e):
         return (e // (ny * nz), (e // nz) % ny, e % nz)
@@ -80,30 +84,28 @@
         else:
             pl.when(cond)(fn)
 
-    far_first = sorted(range(gsize), key=lambda r: -(r % nz))
-
-    def each_peer(fn):
+    def each_of(q, fn):
         for i, (g, ok, _, there) in enumerate(across):
             def outer(i=i, g=g, there=there):
-                for r in far_first:
-                    fn(g * gsize + (rel ^ r), there, i + 1)
+                for k in range(lines):
+                    fn(g * gsize + (own ^ k) * line + q, there, i + 1)
             when(ok, outer)
-        for r in far_first:
-            if r:
-                fn(group * gsize + (rel ^ r), mine, 0)
+        for k in range(lines - 1, 0, -1):
+            fn(group * gsize + (own ^ k) * line + q, mine, 0)
+        pl.when(pos != q)(lambda: fn(group * gsize + own * line + q, mine, 0))
 
     barrier = pltpu.get_barrier_semaphore()
-    each_peer(
-        lambda e, there, i: pl.semaphore_signal(
-            barrier, inc=1, device_id=place(e), device_id_type=MESH
-        )
-    )
-    expected = jnp.int32(gsize - 1)
+
+    def greet(e, *_):
+        pl.semaphore_signal(barrier, inc=1, device_id=place(e), device_id_type=MESH)
+
+    for q in range(line - 1, -1, -1):
+        pl.when(q >= pos)(functools.partial(each_of, q, greet))
+    expected = jnp.int32(lines)
     for _, ok, _, _ in across:
-        expected += gsize if ok is None else gsize * ok.astype(jnp.int32)
-
-    wide_x[leaves + 2 * REACH] = jnp.zeros((rows, leaf), BF16)
-    wide_c[leaves + 2 * REACH] = jnp.zeros((rows, 2 * rank), BF16)
+        expected += lines if ok is None else lines * ok.astype(jnp.int32)
+    expected = expected * (pos + 1) - 1
+
     low = lax.broadcasted_iota(jnp.int32, (rows, 2 * rank), 1) < rank
 
     l_rhs.wait()
@@ -111,46 +113,63 @@
     coeffs = []
     for t in range(leaves):
         block = rhs_v[:, t * leaf:(t + 1) * leaf]
-        wide_x[REACH + t] = block
         basis = basis_v[t]
         both = mm_nt(block, jnp.concatenate([basis, basis], 0)).astype(BF16)
-        wide_c[REACH + t] = both
         coeffs.append(both)
     pairs = [jnp.where(low, coeffs[t], coeffs[t + 1]) for t in range(0, leaves, 2)]
     l_trans.wait()
     root = mm(jnp.concatenate(pairs, 1), trans_v[...].reshape(leaves * rank, rank)).astype(BF16)
-    slots[mine, rel] = jnp.concatenate([root, root], 1)
+    slots[mine, pos, own] = jnp.concatenate([root, root], 1)
 
     pl.semaphore_wait(barrier, expected)
 
-    each_peer(
-        lambda e, there, i: pltpu.make_async_remote_copy(
-            src_ref=slots.at[mine, rel], dst_ref=slots.at[there, rel],
-            send_sem=p_send.at[i], recv_sem=p_recv.at[there],
-            device_id=place(e), device_id_type=MESH,
-        ).start()
-    )
-
-    def halo(buf, i, up):
-        first, land = (leaves, 0) if up else (REACH, leaves + REACH)
+    def send(q):
+        each_of(
+            q,
+            lambda e, there, i: pltpu.make_async_remote_copy(
+                src_ref=slots.at[mine, pos, own], dst_ref=slots.at[there, pos, own],
+                send_sem=p_send.at[i, q], recv_sem=p_recv.at[there, pos],
+                device_id=place(e), device_id_type=MESH,
+            ).start(),
+        )
+
+    def landed(block, q, number, sem):
+        some = slots.at[block, q, pl.ds(0, number)]
+        pltpu.make_async_copy(some, some, sem).wait()
+
+    def arrived(q):
+        pl.when(q == pos)(functools.partial(landed, mine, q, lines - 1, p_recv.at[mine, q]))
+        pl.when(q != pos)(functools.partial(landed, mine, q, lines, p_recv.at[mine, q]))
+        for _, ok, here, _ in across:
+            when(ok, functools.partial(landed, here, q, lines, p_recv.at[here, q]))
+
+    def halo(src, first, dst, land, i, up):
         return pltpu.make_async_remote_copy(
-            src_ref=buf.at[pl.ds(first, REACH)], dst_ref=buf.at[pl.ds(land, REACH)],
+            src_ref=src.at[pl.ds(first, REACH)], dst_ref=dst.at[pl.ds(land, REACH)],
             send_sem=halo_send.at[i], recv_sem=halo_recv.at[i],
             device_id=place(me + 1 if up else me - 1), device_id_type=MESH,
         )
 
-    ups = (halo(wide_c, 0, True), halo(wide_x, 1, True))
-    downs = (halo(wide_c, 2, False), halo(wide_x, 3, False))
-
-    @pl.when(has_next)
-    def _():
-        for copy in ups:
+    ups = (halo(high_c, leaves - REACH, low_c, 0, 0, True),
+           halo(high_x, leaves - REACH, low_x, 0, 1, True))
+    downs = (halo(low_c, REACH, high_c, leaves, 2, False),
+             halo(low_x, REACH, high_x, leaves, 3, False))
+
+    def start(copies):
+        for copy in copies:
             copy.start()
 
-    @pl.when(has_prev)
-    def _():
-        for copy in downs:
-            copy.start()
+    for q in range(line):
+        pl.when(q <= pos)(functools.partial(send, q))
+    for t in range(leaves):
+        for ref, at in ((low_x, REACH + t), (high_x, t)):
+            ref[at] = rhs_v[:, t * leaf:(t + 1) * leaf]
+        for ref, at in ((low_c, REACH + t), (high_c, t)):
+            ref[at] = coeffs[t]
+    for ref in (low_x, high_x, low_c, high_c):
+        ref[leaves + REACH] = jnp.zeros(ref.shape[1:], BF16)
+    pl.when(has_next & (pos == line - 1))(functools.partial(start, ups))
+    pl.when(has_prev & (pos > 0))(functools.partial(start, downs))
 
     l_top.wait()
     l_cc.wait()
@@ -165,9 +184,9 @@
     reach_mats = []
     for h in range(topl + 1):
         if h == 1:
-            down = top_v[0, rel % 2]
+            down = top_v[0, me % 2]
         elif h > 1:
-            down = mm(down, top_v[h - 1, (rel // 2 ** (h - 1)) % 2]).astype(BF16)
+            down = mm(down, top_v[h - 1, (me // 2 ** (h - 1)) % 2]).astype(BF16)
         reach_mats.append(
             mm_nt(cc_v[h].reshape(2 * rank, rank), jnp.concatenate([down] * blocks, 0))
         )
@@ -198,48 +217,59 @@
     l_nsrc.wait()
     l_coup.wait()
     l_near.wait()
-
-    @pl.when(has_prev)
-    def _():
-        for copy in ups:
-            copy.wait_recv()
-
-    @pl.when(has_next)
-    def _():
-        for copy in downs:
-            copy.wait_recv()
-
-    anchor = me * leaves - REACH
-    last = leaves + 2 * REACH
-
-    def spot(source):
-        return jnp.where(source >= 0, jnp.clip(source - anchor, 0, last - 1), last)
-
-    sums = []
-    for t in range(leaves):
+    sums = [
+        mm(rhs_v[:, t * leaf:(t + 1) * leaf], near_v[t, 0]) for t in range(leaves)
+    ]
+
+    def meet(q):
+        arrived(q)
+        send(q)
+        if q == line - 1:
+            pl.when(has_prev & (pos == 0))(functools.partial(start, downs))
+        pl.when(has_next & (pos == q - 1))(functools.partial(start, ups))
+
+    def neighbours(t, wide_x, wide_c, anchor):
+        def spot(source):
+            inside = jnp.clip(source - anchor, 0, leaves + REACH - 1)
+            return jnp.where(source >= 0, inside, leaves + REACH)
+
         picked = [wide_c[spot(csrc_s[t, a])] for a in range(slots_adm)]
         picked = [jnp.where(low, picked[a], picked[a + 1]) for a in range(0, slots_adm, 2)]
         field = mm(
             jnp.concatenate(picked, 1), coup_v[t].reshape(slots_adm * rank, rank)
         ).astype(BF16)
-        inputs = [wide_x[REACH + t]]
-        inputs += [wide_x[spot(nsrc_s[t, n])] for n in range(1, slots_near)]
-        sums.append(
-            mm(jnp.concatenate(inputs, 1), near_v[t].reshape(slots_near * leaf, leaf))
-            + mm(field, basis_v[t])
-        )
-
-    def landed(block, number, sem):
-        group_slots = slots.at[block, pl.ds(0, number)]
-        pltpu.make_async_copy(group_slots, group_slots, sem).wait()
-
-    landed(mine, gsize - 1, p_recv.at[mine])
-    for _, ok, here, _ in across:
-        when(ok, functools.partial(landed, here, gsize, p_recv.at[here]))
+        inputs = [wide_x[spot(nsrc_s[t, n])] for n in range(1, slots_near)]
+        return mm(jnp.concatenate(inputs, 1), near_v[t, 1:].reshape(-1, leaf)) + mm(
+            field, basis_v[t]
+        )
+
+    def receive(copies):
+        for copy in copies:
+            copy.wait_recv()
+
+    for q in range(1, line - 1):
+        pl.when(q > pos)(functools.partial(meet, q))
+
+    pl.when(has_next)(functools.partial(receive, downs))
+    for t in range(REACH, leaves):
+        sums[t] += neighbours(t, high_x, high_c, me * leaves)
+
+    pl.when(line - 1 > pos)(functools.partial(meet, line - 1))
+
+    pl.when(has_prev)(functools.partial(receive, ups))
+    for t in range(REACH):
+        sums[t] += neighbours(t, low_x, low_c, me * leaves - REACH)
+
+    for q in range(line):
+        pl.when(q <= pos)(functools.partial(arrived, q))
     used = 2 if groups == 2 else 3
     held = [
         jnp.concatenate(
-            [jnp.where(low, slots[b, c], slots[b, c + 1]) for c in range(0, gsize, 2)], 1
+            [
+                jnp.where(low, slots[b, c % line, c // line], slots[b, c % line + 1, c // line])
+                for c in range(0, gsize, 2)
+            ],
+            1,
         )
         for b in range(used)
     ]
@@ -257,9 +287,11 @@
             sums[t] + far[:, t * leaf:(t + 1) * leaf]
         ).astype(BF16)
 
-    landed(mine, gsize - 1, p_send.at[0])
-    for i, (_, ok, here, _) in enumerate(across):
-        when(ok, functools.partial(landed, here, gsize, p_send.at[i + 1]))
+    for q in range(line):
+        pl.when(q == pos)(functools.partial(landed, mine, q, lines - 1, p_send.at[0, q]))
+        pl.when(q != pos)(functools.partial(landed, mine, q, lines, p_send.at[0, q]))
+        for i, (_, ok, here, _) in enumerate(across):
+            when(ok, functools.partial(landed, here, q, lines, p_send.at[i + 1, q]))
 
     @pl.when(has_next)
     def _():
@@ -294,10 +326,12 @@
             in_specs=[pl.BlockSpec(memory_space=pl.ANY)] * len(args),
             out_specs=pl.BlockSpec(memory_space=pltpu.VMEM),
             scratch_shapes=[room(x) for x in args] + [
-                pltpu.VMEM((leaves + 2 * REACH + 1, rows, leaf), BF16),
-                pltpu.VMEM((leaves + 2 * REACH + 1, rows, 2 * rank), BF16),
-                pltpu.VMEM((blocks, gsize, rows, 2 * rank), BF16),
-                dma((len(args),)), dma((4,)), dma((4,)), dma((3,)), dma((blocks,)),
+                pltpu.VMEM((leaves + REACH + 1, rows, leaf), BF16),
+                pltpu.VMEM((leaves + REACH + 1, rows, 2 * rank), BF16),
+                pltpu.VMEM((leaves + REACH + 1, rows, leaf), BF16),
+                pltpu.VMEM((leaves + REACH + 1, rows, 2 * rank), BF16),
+                pltpu.VMEM((blocks, 2**LOW, gsize // 2**LOW, rows, 2 * rank), BF16),
+                dma((len(args),)), dma((4,)), dma((4,)), dma((3, 2**LOW)), dma((blocks, 2**LOW)),
             ],
             compiler_params=pltpu.CompilerParams(collective_id=0, has_side_effects=True),
         )(*(pltpu.with_memory_space_constraint(x, pltpu.HBM) for x in args))

time: 13.4 us -> 15.7 us (1.17)
  the two profiles are of different devices: /device:TPU:0 before, /device:TPU:25 now
where the time goes in v6:
time: 15.7 us; the launch traced here: 15.5 us
  Pallas kernels  14.9 us (95%)
  local copies, waits for them, and re-layouts  0.62 us (4%)
    pallas_call x1, Pallas kernels, local(): pl.pallas_call(functools.partial(kernel, shape), out_shape=pltpu.VMEM(rhs...  14.9 us
    unnamed x1, local copies, waits for them, and re-layouts  0.62 us

profile of v6, /device:TPU:25, one launch (start us, length us, event | category | flops | bytes accessed | tf_op | source)
XLA Modules:
  0.0 15.5 jit_solution(10382412789928567397)
XLA Ops:
  0.0 14.9 %shard_map.91 = bf16[16,1024]{1,0:T(8,128)(2,1)S(1)} custom-call(bf16[16,1024]{1,0:T(8,128)(2,1)} %rhs_h.1, bf16[4,64,256]{2,1,0:T(8,128)(2,1)} %basis_h.1, bf16[4,64,64]{2,1,0:T(8,128)(2,1)} %trans_h.1, bf16[4,6,64,64]{3,2,1,0:T(8,128)(2,1)} %coup_h.1, s32[4,6]{1,0:T(4,128)} %csrc_h.1, bf16[4,3,256,256]{3,2,1,0:T(8,128)(2,1)} %near_h.1, s32[4,3]{1,0:T(4,128)} %nsrc_h.1, ...), custom_call_target="tpu_custom_call" | custom-call | tf_op jit(solution)/shard_map/pallas_call | solution.py:323
  14.9 0.6 %copy.11 = bf16[16,1024]{1,0:T(8,128)(2,1)} copy(bf16[16,1024]{1,0:T(8,128)(2,1)S(1)} %shard_map.91) | data formatting | bytes 65536

commit v7 on v4

--- a/solution.py
+++ b/solution.py
@@ -66,7 +66,8 @@
         )
     ):
         load = pltpu.make_async_copy(src, dst, local_sem.at[i])
-        load.start()
+        if i < 3:
+            load.start()
         loads.append(load)
     (l_rhs, l_basis, l_trans, l_top, l_cc, l_csrc, l_nsrc, l_coup, l_near) = loads
 
@@ -84,7 +85,15 @@
         else:
             pl.when(cond)(fn)
 
-    mates = [mine_line * line + (rel ^ r) for r in range(line - 1, 0, -1)]
+    def to_mate(q):
+        return pltpu.make_async_remote_copy(
+            src_ref=slots.at[rel], dst_ref=slots.at[rel],
+            send_sem=p_send.at[q], recv_sem=p_recv.at[rel],
+            device_id=place(mine_line * line + q), device_id_type=MESH,
+        )
+
+    def from_mate(q):
+        return pltpu.make_async_copy(slots.at[q], slots.at[q], p_recv.at[q])
 
     def each_line(fn):
         for i, (g, ok, here, there) in enumerate(across):
@@ -102,15 +111,13 @@
     def greet(e, *_):
         pl.semaphore_signal(barrier, inc=1, device_id=place(e), device_id_type=MESH)
 
-    for e in mates:
-        greet(e)
+    for r in range(line - 1, 0, -1):
+        pl.when((rel ^ r) > rel)(functools.partial(greet, mine_line * line + (rel ^ r)))
     out_prev = has_prev & (rel == 0)
     out_next = has_next & (rel == line - 1)
     when(out_prev, functools.partial(greet, me - 1))
-    when(out_next, functools.partial(greet, me + 1))
     each_line(greet)
-    expected = jnp.int32(line - 1 + lines - 1)
-    expected += out_prev.astype(jnp.int32) + out_next.astype(jnp.int32)
+    expected = rel + lines - 1 + out_next.astype(jnp.int32)
     for _, ok, _, _ in across:
         expected += lines if ok is None else lines * ok.astype(jnp.int32)
 
@@ -147,23 +154,22 @@
     def send():
         pl.semaphore_wait(barrier, expected)
 
-        for e in mates:
-            pltpu.make_async_remote_copy(
-                src_ref=slots.at[rel], dst_ref=slots.at[rel],
-                send_sem=p_send.at[0], recv_sem=p_recv.at[0],
-                device_id=place(e), device_id_type=MESH,
-            ).start()
-        @pl.when(has_next)
+        for q in range(line):
+            pl.when(q < rel)(lambda q=q: to_mate(q).start())
+
+        @pl.when(out_next)
         def _():
             for copy in ups:
                 copy.start()
 
-        @pl.when(has_prev)
+        @pl.when(rel > 0)
         def _():
             for copy in downs:
                 copy.start()
 
     def prepare():
+        for load in loads[3:]:
+            load.start()
         l_top.wait()
         l_cc.wait()
         lane_block = lax.broadcasted_iota(jnp.int32, (1, width), 1) // rank
@@ -228,11 +234,23 @@
         some = buf.at[pl.ds(0, number)]
         pltpu.make_async_copy(some, some, sem).wait()
 
-    landed(slots, line - 1, p_recv.at[0])
+    for q in range(1, line):
+        @pl.when(q > rel)
+        def _(q=q):
+            from_mate(q).wait()
+            to_mate(q).start()
+
+        @pl.when(q - 1 == rel)
+        def _():
+            for copy in ups:
+                copy.start()
+
+    for q in range(line):
+        pl.when(q < rel)(lambda q=q: from_mate(q).wait())
     held = [jnp.where(low, slots[c], slots[c + 1]) for c in range(0, line, 2)]
     parts = mm(jnp.concatenate(held, 1), gather_v[...])
     for i in range(part.shape[0]):
-        part[i] = parts[:, i * 2 * rank:(i + 1) * 2 * rank]
+        part[i] = parts[:, i * 2 * rank:(i + 1) * 2 * rank].astype(BF16)
     each_line(
         lambda e, here, l, there, i: pltpu.make_async_remote_copy(
             src_ref=part.at[here * (lines // 2) + l // 2], dst_ref=part_in.at[there * lines + own],
@@ -250,6 +268,11 @@
     def _():
         for copy in ups:
             copy.wait_recv()
+
+    @pl.when(out_prev)
+    def _():
+        for copy in downs:
+            copy.start()
 
     @pl.when(has_next)
     def _():
@@ -281,7 +304,7 @@
         when(ok, functools.partial(landed, part_in, lines, r_recv.at[here]))
     total = jnp.zeros((rows, 2 * rank), F32)
     for j in range(part_in.shape[0]):
-        term = part_in[j]
+        term = part_in[j].astype(F32)
         if groups != 2 and j // lines != 1:
             term = jnp.where(group > 0 if j < lines else group < groups - 1, term, 0.0)
         total += term
@@ -292,7 +315,8 @@
             sums[t] + far[:, t * leaf:(t + 1) * leaf]
         ).astype(BF16)
 
-    landed(slots, line - 1, p_send.at[0])
+    for q in range(line):
+        pl.when(q != rel)(lambda q=q: to_mate(q).wait_send())
     landed(part_in, lines - 1, r_send.at[0])
     for i, (_, ok, _, _) in enumerate(across):
         when(ok, functools.partial(landed, part_in, lines, r_send.at[i + 1]))
@@ -333,12 +357,12 @@
                 pltpu.VMEM((leaves + 2 * REACH + 1, rows, leaf), BF16),
                 pltpu.VMEM((leaves + 2 * REACH + 1, rows, 2 * rank), BF16),
                 pltpu.VMEM((2**LOW, rows, 2 * rank), BF16),
-                pltpu.VMEM((lines // 2, rows, 2 * rank), F32),
-                pltpu.VMEM((lines, rows, 2 * rank), F32),
+                pltpu.VMEM((lines // 2, rows, 2 * rank), BF16),
+                pltpu.VMEM((lines, rows, 2 * rank), BF16),
                 pltpu.VMEM((2**LOW * rank, lines * rank), BF16),
                 pltpu.VMEM((2 * rank, leaves * leaf), BF16),
                 pltpu.VMEM((rows, leaves * leaf), F32),
-                dma((len(args),)), dma((4,)), dma((4,)), dma((1,)), dma((1,)),
+                dma((len(args),)), dma((4,)), dma((4,)), dma((2**LOW,)), dma((2**LOW,)),
                 dma((3,)), dma((3,)),
             ],
             compiler_params=pltpu.CompilerParams(collective_id=0, has_side_effects=True),

time: 13.5 us -> 14.9 us (1.10)
  the two profiles are of different devices: /device:TPU:0 before, /device:TPU:17 now
where the time goes in v7:
time: 14.9 us; the launch traced here: 14.8 us
  Pallas kernels  14.2 us (95%)
  local copies, waits for them, and re-layouts  0.62 us (4%)
    pallas_call x1, Pallas kernels, local(): pl.pallas_call(functools.partial(kernel, shape), out_shape=pltpu.VMEM(rhs...  14.2 us
    unnamed x1, local copies, waits for them, and re-layouts  0.62 us

profile of v7, /device:TPU:17, one launch (start us, length us, event | category | flops | bytes accessed | tf_op | source)
XLA Modules:
  0.0 14.8 jit_solution(14216782348620281883)
XLA Ops:
  0.0 14.2 %shard_map.91 = bf16[16,1024]{1,0:T(8,128)(2,1)S(1)} custom-call(bf16[16,1024]{1,0:T(8,128)(2,1)} %rhs_h.1, bf16[4,64,256]{2,1,0:T(8,128)(2,1)} %basis_h.1, bf16[4,64,64]{2,1,0:T(8,128)(2,1)} %trans_h.1, bf16[4,6,64,64]{3,2,1,0:T(8,128)(2,1)} %coup_h.1, s32[4,6]{1,0:T(4,128)} %csrc_h.1, bf16[4,3,256,256]{3,2,1,0:T(8,128)(2,1)} %near_h.1, s32[4,3]{1,0:T(4,128)} %nsrc_h.1, ...), custom_call_target="tpu_custom_call" | custom-call | tf_op jit(solution)/shard_map/pallas_call | solution.py:351
  14.2 0.6 %copy.11 = bf16[16,1024]{1,0:T(8,128)(2,1)} copy(bf16[16,1024]{1,0:T(8,128)(2,1)S(1)} %shard_map.91) | data formatting | bytes 65536

commit v8 on v7

--- a/solution.py
+++ b/solution.py
@@ -221,7 +221,7 @@
         for t in range(leaves):
             first_v[:, t * leaf:(t + 1) * leaf] = mm(wide_x[REACH + t], near_v[t, 0])
 
-    turn = jnp.where(rel < line // 2, 0, 1)
+    turn = jnp.where(rel == 0, 0, 1)
 
     def step(i, carry):
         pl.when(i == turn)(prepare)

time: 14.9 us -> 14.1 us (0.946)
  the two profiles are of different devices: /device:TPU:17 before, /device:TPU:25 now
where the time goes in v8:
time: 14.1 us; the launch traced here: 13.9 us
  Pallas kernels  13.3 us (94%)
  local copies, waits for them, and re-layouts  0.62 us (4%)
    pallas_call x1, Pallas kernels, local(): pl.pallas_call(functools.partial(kernel, shape), out_shape=pltpu.VMEM(rhs...  13.3 us
    unnamed x1, local copies, waits for them, and re-layouts  0.62 us

profile of v8, /device:TPU:25, one launch (start us, length us, event | category | flops | bytes accessed | tf_op | source)
XLA Modules:
  0.0 13.9 jit_solution(10534365899774956279)
XLA Ops:
  0.0 13.3 %shard_map.91 = bf16[16,1024]{1,0:T(8,128)(2,1)S(1)} custom-call(bf16[16,1024]{1,0:T(8,128)(2,1)} %rhs_h.1, bf16[4,64,256]{2,1,0:T(8,128)(2,1)} %basis_h.1, bf16[4,64,64]{2,1,0:T(8,128)(2,1)} %trans_h.1, bf16[4,6,64,64]{3,2,1,0:T(8,128)(2,1)} %coup_h.1, s32[4,6]{1,0:T(4,128)} %csrc_h.1, bf16[4,3,256,256]{3,2,1,0:T(8,128)(2,1)} %near_h.1, s32[4,3]{1,0:T(4,128)} %nsrc_h.1, ...), custom_call_target="tpu_custom_call" | custom-call | tf_op jit(solution)/shard_map/pallas_call | solution.py:351
  13.3 0.6 %copy.11 = bf16[16,1024]{1,0:T(8,128)(2,1)} copy(bf16[16,1024]{1,0:T(8,128)(2,1)S(1)} %shard_map.91) | data formatting | bytes 65536

commit v9 on v4

--- a/solution.py
+++ b/solution.py
@@ -66,7 +66,8 @@
         )
     ):
         load = pltpu.make_async_copy(src, dst, local_sem.at[i])
-        load.start()
+        if i < 3:
+            load.start()
         loads.append(load)
     (l_rhs, l_basis, l_trans, l_top, l_cc, l_csrc, l_nsrc, l_coup, l_near) = loads
 
@@ -164,6 +165,8 @@
                 copy.start()
 
     def prepare():
+        for load in loads[3:]:
+            load.start()
         l_top.wait()
         l_cc.wait()
         lane_block = lax.broadcasted_iota(jnp.int32, (1, width), 1) // rank
@@ -232,7 +235,7 @@
     held = [jnp.where(low, slots[c], slots[c + 1]) for c in range(0, line, 2)]
     parts = mm(jnp.concatenate(held, 1), gather_v[...])
     for i in range(part.shape[0]):
-        part[i] = parts[:, i * 2 * rank:(i + 1) * 2 * rank]
+        part[i] = parts[:, i * 2 * rank:(i + 1) * 2 * rank].astype(BF16)
     each_line(
         lambda e, here, l, there, i: pltpu.make_async_remote_copy(
             src_ref=part.at[here * (lines // 2) + l // 2], dst_ref=part_in.at[there * lines + own],
@@ -281,7 +284,7 @@
         when(ok, functools.partial(landed, part_in, lines, r_recv.at[here]))
     total = jnp.zeros((rows, 2 * rank), F32)
     for j in range(part_in.shape[0]):
-        term = part_in[j]
+        term = part_in[j].astype(F32)
         if groups != 2 and j // lines != 1:
             term = jnp.where(group > 0 if j < lines else group < groups - 1, term, 0.0)
         total += term
@@ -333,8 +336,8 @@
                 pltpu.VMEM((leaves + 2 * REACH + 1, rows, leaf), BF16),
                 pltpu.VMEM((leaves + 2 * REACH + 1, rows, 2 * rank), BF16),
                 pltpu.VMEM((2**LOW, rows, 2 * rank), BF16),
-                pltpu.VMEM((lines // 2, rows, 2 * rank), F32),
-                pltpu.VMEM((lines, rows, 2 * rank), F32),
+                pltpu.VMEM((lines // 2, rows, 2 * rank), BF16),
+                pltpu.VMEM((lines, rows, 2 * rank), BF16),
                 pltpu.VMEM((2**LOW * rank, lines * rank), BF16),
                 pltpu.VMEM((2 * rank, leaves * leaf), BF16),
                 pltpu.VMEM((rows, leaves * leaf), F32),

time: 13.5 us -> 13.8 us (1.022)
  Pallas kernels: 12.7 us -> 13.1 us
    pallas_call x1, Pallas kernels: 12.7 us -> 13.1 us  [local(): pl.pallas_call(functools.partial(kernel, shape), out_shape=pltpu.VMEM(rhs...]
where the time goes in v9:
time: 13.8 us; the launch traced here: 13.7 us
  Pallas kernels  13.1 us (95%)
  local copies, waits for them, and re-layouts  0.62 us (4%)
    pallas_call x1, Pallas kernels, local(): pl.pallas_call(functools.partial(kernel, shape), out_shape=pltpu.VMEM(rhs...  13.1 us
    unnamed x1, local copies, waits for them, and re-layouts  0.62 us

profile of v9, /device:TPU:0, one launch (start us, length us, event | category | flops | bytes accessed | tf_op | source)
XLA Modules:
  0.0 13.7 jit_solution(6260272278868519268)
XLA Ops:
  0.0 13.1 %shard_map.91 = bf16[16,1024]{1,0:T(8,128)(2,1)S(1)} custom-call(bf16[16,1024]{1,0:T(8,128)(2,1)} %rhs_h.1, bf16[4,64,256]{2,1,0:T(8,128)(2,1)} %basis_h.1, bf16[4,64,64]{2,1,0:T(8,128)(2,1)} %trans_h.1, bf16[4,6,64,64]{3,2,1,0:T(8,128)(2,1)} %coup_h.1, s32[4,6]{1,0:T(4,128)} %csrc_h.1, bf16[4,3,256,256]{3,2,1,0:T(8,128)(2,1)} %near_h.1, s32[4,3]{1,0:T(4,128)} %nsrc_h.1, ...), custom_call_target="tpu_custom_call" | custom-call | tf_op jit(solution)/shard_map/pallas_call | solution.py:330
  13.1 0.6 %copy.11 = bf16[16,1024]{1,0:T(8,128)(2,1)} copy(bf16[16,1024]{1,0:T(8,128)(2,1)S(1)} %shard_map.91) | data formatting | bytes 65536
